TPU v7x, 512 devices: a whole 4x8x8 slice. The times are simulated.
512 devices in a mesh: slab: 128 (over x_lo, z, y), rep: 4 (over x_hi, core).
Axes of the slice: x: 4 (x_hi: 2, x_lo: 2; x = x_hi * 2 + x_lo), y: 8, z: 8, core: 2. Of those that a mesh axis runs over, the one named last changes fastest.
Arguments:
- saved_input: bfloat16 [4, 6, 1, 256, 256, 256], P('rep', None, None, 'slab'), may hold values from -6 to 6
- output_grad: bfloat16 [4, 6, 1, 256, 256, 256], P('rep', None, None, 'slab'), may hold values from -6 to 6
- spectral_weight: float32 [1024, 8, 1, 1, 32], P('slab'), may hold values from -18 to 18
- bypass_weight: float32 [8, 1, 1], replicated, may hold values from -1.8 to 1.8
Outputs:
- input_grad: bfloat16 [4, 6, 1, 256, 256, 256], P('rep', None, None, 'slab')
- weight_grad: float32 [1024, 8, 1, 1, 32], P('slab')
All inputs are finite; a program needn't handle non-finite values.
Results may differ from a plain program's by a relative error of at most 0.001.
Values sent between devices are 32-bit elements; how exact they have to be, the bound alone decides.
No kernel may reach another device: no remote copies, remote signals or barrier semaphores. Data moves between devices by JAX's collectives and lax.ppermute only.
A program may use at most 64 MiB of HBM per device.

v0:
```python
import math

import jax
import jax.numpy as jnp
from jax import lax
from jax.sharding import PartitionSpec as P

NZ = 256
KM = 32


HIGHEST_PRECISION = lax.Precision.HIGHEST


def frequencies(number):
    counter = lax.iota(jnp.int32, number)
    return jnp.where(counter < number // 2, counter, counter - number)


def phase_table(positions, number, length):
    phases = positions[:, None] * frequencies(number)[None, :] % length
    angles = phases.astype(jnp.float32) * (2.0 * math.pi / length)
    return (jnp.cos(angles), jnp.sin(angles))


def cross_three(left, right):
    return (
        left[1] * right[2] - left[2] * right[1],
        left[2] * right[0] - left[0] * right[2],
        left[0] * right[1] - left[1] * right[0],
    )


def cross_pair(left_real, left_imag, right_real, right_imag):
    first = cross_three(left_real, right_real)
    second = cross_three(left_imag, right_imag)
    third = cross_three(left_real, right_imag)
    fourth = cross_three(left_imag, right_real)
    real_part = tuple((first[axis_id] - second[axis_id] for axis_id in range(3)))
    imag_part = tuple((third[axis_id] + fourth[axis_id] for axis_id in range(3)))
    return (real_part, imag_part)


def adjoint_product(scalar_real, scalar_imag, vector_real, vector_imag, grad_real, grad_imag):
    cross_real, cross_imag = cross_pair(
        vector_real, tuple((-entry for entry in vector_imag)), grad_real, grad_imag
    )
    real_part = tuple(
        (
            scalar_real * grad_real[axis_id]
            + scalar_imag * grad_imag[axis_id]
            - cross_imag[axis_id]
            for axis_id in range(3)
        )
    )
    imag_part = tuple(
        (
            scalar_real * grad_imag[axis_id]
            - scalar_imag * grad_real[axis_id]
            + cross_real[axis_id]
            for axis_id in range(3)
        )
    )
    return (real_part, imag_part)


def plane_modes(fields, factor):
    count_first, count_second = (fields.shape[3], fields.shape[4])
    half_comps = fields.shape[1] // 2
    cosine_second, sine_second = phase_table(lax.iota(jnp.int32, count_second), KM, count_second)
    cosine_first, sine_first = phase_table(lax.iota(jnp.int32, count_first), KM, count_first)
    tables_second = jnp.concatenate([cosine_second, sine_second], axis=1)
    along_second = jnp.einsum("fczxy,yk->fczxk", fields, tables_second, precision=HIGHEST_PRECISION)
    real_part = along_second[:, :half_comps, :, :, :KM] + along_second[:, half_comps:, :, :, KM:]
    imag_part = along_second[:, half_comps:, :, :, :KM] - along_second[:, :half_comps, :, :, KM:]
    stacked = jnp.concatenate([real_part, imag_part], axis=1)
    with_cos = jnp.einsum("fczxk,xm->fczmk", stacked, cosine_first, precision=HIGHEST_PRECISION)
    with_sin = jnp.einsum("fczxk,xm->fczmk", stacked, sine_first, precision=HIGHEST_PRECISION)
    real_part = with_cos[:, :half_comps] + with_sin[:, half_comps:]
    imag_part = with_cos[:, half_comps:] - with_sin[:, :half_comps]
    modes = jnp.concatenate([real_part, imag_part], axis=1) * factor
    return modes.reshape(modes.shape[0], fields.shape[1], modes.shape[2], KM * KM)


def depth_forward(block, cosine_depth, sine_depth):
    half_comps = block.shape[1] // 2
    with_cos = jnp.einsum("fczr,zk->rfck", block, cosine_depth, precision=HIGHEST_PRECISION)
    with_sin = jnp.einsum("fczr,zk->rfck", block, sine_depth, precision=HIGHEST_PRECISION)
    real_part = with_cos[:, :, :half_comps] + with_sin[:, :, half_comps:]
    imag_part = with_cos[:, :, half_comps:] - with_sin[:, :, :half_comps]
    return jnp.concatenate([real_part, imag_part], axis=2)


def depth_inverse(rows_block, cosine_depth, sine_depth):
    half_comps = rows_block.shape[1] // 2
    with_cos = jnp.einsum("rck,zk->czr", rows_block, cosine_depth, precision=HIGHEST_PRECISION)
    with_sin = jnp.einsum("rck,zk->czr", rows_block, sine_depth, precision=HIGHEST_PRECISION)
    real_part = with_cos[:half_comps] - with_sin[half_comps:]
    imag_part = with_cos[half_comps:] + with_sin[:half_comps]
    return jnp.concatenate([real_part, imag_part], axis=0)


def shards(saved_input, output_grad, spectral_weight, bypass_weight):
    channels = saved_input.shape[2]
    planes, count_first, count_second = (
        saved_input.shape[3],
        saved_input.shape[4],
        saved_input.shape[5],
    )
    components = 6 * channels
    half_comps = 3 * channels
    factor = 1.0 / math.sqrt(count_first * count_second * NZ)
    rows_owned = spectral_weight.shape[0]
    fields = jnp.concatenate([saved_input, output_grad], axis=0).astype(jnp.float32)
    fields = fields.reshape(2, components, planes, count_first, count_second)
    modes = plane_modes(fields, factor)
    slab_start = lax.axis_index("slab") * planes
    cosine_depth, sine_depth = phase_table(slab_start + lax.iota(jnp.int32, planes), KM, NZ)
    spectra = lax.psum_scatter(
        depth_forward(modes, cosine_depth, sine_depth), "slab", scatter_dimension=0, tiled=True
    )
    parts = spectra.reshape(rows_owned, 2, 2, 3, channels, KM)
    inputs_real = tuple((parts[:, 0, 0, axis_id][:, None] for axis_id in range(3)))
    inputs_imag = tuple((parts[:, 0, 1, axis_id][:, None] for axis_id in range(3)))
    grads_real = tuple((parts[:, 1, 0, axis_id][:, :, None] for axis_id in range(3)))
    grads_imag = tuple((parts[:, 1, 1, axis_id][:, :, None] for axis_id in range(3)))
    scalar_real = sum(
        (
            inputs_real[axis_id] * grads_real[axis_id] + inputs_imag[axis_id] * grads_imag[axis_id]
            for axis_id in range(3)
        )
    )
    scalar_imag = sum(
        (
            inputs_real[axis_id] * grads_imag[axis_id] - inputs_imag[axis_id] * grads_real[axis_id]
            for axis_id in range(3)
        )
    )
    cross_real, cross_imag = cross_pair(
        inputs_real, tuple((-entry for entry in inputs_imag)), grads_real, grads_imag
    )
    local_grad = jnp.stack(
        [scalar_real] + list(cross_imag) + [scalar_imag] + [-entry for entry in cross_real], axis=1
    )
    weight_grad = lax.psum(local_grad, "rep")
    weight_vector_real = tuple((spectral_weight[:, 1 + axis_id] for axis_id in range(3)))
    weight_vector_imag = tuple((spectral_weight[:, 5 + axis_id] for axis_id in range(3)))
    mode_real, mode_imag = adjoint_product(
        spectral_weight[:, 0],
        spectral_weight[:, 4],
        weight_vector_real,
        weight_vector_imag,
        grads_real,
        grads_imag,
    )
    mode_grads = jnp.stack(
        [jnp.sum(entry, axis=1) for entry in list(mode_real) + list(mode_imag)], axis=1
    )
    mode_grads = mode_grads.reshape(rows_owned, components, KM)
    depth_modes = depth_inverse(
        lax.all_gather(mode_grads, "slab", axis=0, tiled=True), cosine_depth, sine_depth
    )
    cosine_second, sine_second = phase_table(lax.iota(jnp.int32, count_second), KM, count_second)
    cosine_first, sine_first = phase_table(lax.iota(jnp.int32, count_first), KM, count_first)
    grid_modes = depth_modes.reshape(components, planes, KM, KM)
    with_cos = jnp.einsum("czmk,xm->czxk", grid_modes, cosine_first, precision=HIGHEST_PRECISION)
    with_sin = jnp.einsum("czmk,xm->czxk", grid_modes, sine_first, precision=HIGHEST_PRECISION)
    stacked = jnp.concatenate(
        [
            with_cos[:half_comps] - with_sin[half_comps:],
            with_cos[half_comps:] + with_sin[:half_comps],
        ],
        axis=0,
    )
    with_cos = jnp.einsum("czxk,yk->czxy", stacked, cosine_second, precision=HIGHEST_PRECISION)
    with_sin = jnp.einsum("czxk,yk->czxy", stacked, sine_second, precision=HIGHEST_PRECISION)
    spectral_real = (with_cos[:half_comps] - with_sin[half_comps:]) * factor
    spectral_imag = (with_cos[half_comps:] + with_sin[:half_comps]) * factor
    cotangent = fields[1].reshape(2, 3, channels, planes, count_first, count_second)
    field_real = tuple((cotangent[0, axis_id][:, None] for axis_id in range(3)))
    field_imag = tuple((cotangent[1, axis_id][:, None] for axis_id in range(3)))

    def expand(entry):
        return entry[:, :, None, None, None]

    bypass_vector_real = tuple((expand(bypass_weight[1 + axis_id]) for axis_id in range(3)))
    bypass_vector_imag = tuple((expand(bypass_weight[5 + axis_id]) for axis_id in range(3)))
    bypass_real, bypass_imag = adjoint_product(
        expand(bypass_weight[0]),
        expand(bypass_weight[4]),
        bypass_vector_real,
        bypass_vector_imag,
        field_real,
        field_imag,
    )
    bypass_real = jnp.stack([jnp.sum(entry, axis=0) for entry in bypass_real], axis=0).reshape(
        half_comps, planes, count_first, count_second
    )
    bypass_imag = jnp.stack([jnp.sum(entry, axis=0) for entry in bypass_imag], axis=0).reshape(
        half_comps, planes, count_first, count_second
    )
    total_real = spectral_real + bypass_real
    total_imag = spectral_imag + bypass_imag
    input_grad = jnp.concatenate([total_real, total_imag], axis=0).astype(jnp.bfloat16)
    input_grad = input_grad.reshape(1, 6, channels, planes, count_first, count_second)
    return (input_grad, weight_grad)


def solution(mesh):
    placed = (
        P("rep", None, None, "slab", None, None),
        P("rep", None, None, "slab", None, None),
        P("slab", None, None, None, None),
        P(),
    )
    return jax.shard_map(
        shards,
        mesh=mesh,
        in_specs=placed,
        out_specs=(P("rep", None, None, "slab", None, None), P("slab", None, None, None, None)),
        check_vma=False,
    )
```

profile of v0, /device:TPU:1, one launch (start us, length us, event | category | flops | bytes accessed | tf_op | source)
XLA Modules:
  0.0 1615.9 jit_solution(18340750350543128587)
XLA Ops:
  7.2 0.0 all-reduce.3.cloned.1.call-start
  7.2 0.2 fusion.30
  7.4 4.9 fusion
  12.3 0.1 slice_add_fusion.2
  12.4 2.1 convolution_bitcast_fusion.4
  14.5 2.1 convolution_bitcast_fusion.5
  16.6 0.1 slice_add_fusion.4
  16.6 0.1 concatenate.52
  16.8 0.1 concatenate.53
  16.9 1.6 convolution_bitcast_fusion.1
  18.5 1.6 convolution_bitcast_fusion
  20.1 0.4 slice_add_fusion.1
  20.4 0.2 pad_maximum_fusion
  20.6 6.8 copy.37
  27.4 0.0 copy-start.1
  27.4 0.0 all-reduce.3.cloned.1.call-update
  27.5 0.6 copy-done.1
  28.1 0.7 fusion.120
  30.1 0.0 copy-start
  30.1 1.7 convert.12
  32.5 1.3 dynamic-slice
  34.6 0.0 copy-done
  34.6 3.9 subtract_bitcast_fusion.1
  38.5 3.8 subtract_bitcast_fusion.2
  42.3 3.7 subtract_bitcast_fusion
  46.0 1113.0 %all-reduce.3.cloned.1.call-done = f32[1024,2,6,32]{3,1,2,0:T(2,128)} async-done(((f32[1024,2,6,32]{3,1,2,0:T(2,128)}), f32[1024,2,6,32]{3,1,2,0:T(2,128)}) %all-reduce.3.cloned.1.call-update) | async-done | bytes 1572880
  1159.0 0.8 constant_dynamic-slice_fusion
  1160.0 266.6 %all-gather = f32[1024,6,1,32]{3,2,1,0:T(1,128)S(1)} all-gather(f32[8,6,1,32]{3,2,1,0:T(1,128)S(1)} %copy.51), channel_id=2, replica_groups=mesh['slab'=128,'rep'=4] {'slab'}, dimensions={0}, use_global_device_ids=true | all-gather | bytes 792576 | tf_op jit(solution)/shard_map/all_gather | solution.py:161
  1426.6 5.8 copy.52
  1432.4 1.7 convolution_bitcast_fusion.7
  1434.1 1.7 convolution_bitcast_fusion.6
  1435.9 0.1 reshape.2626
  1436.0 0.7 convolution_bitcast_fusion.3
  1436.7 0.7 convolution_bitcast_fusion.2
  1437.4 0.1 slice_subtract_fusion.3
  1437.4 2.8 fusion.14
  1440.2 4.4 fusion.13
  1444.7 0.1 stack.11
  1444.7 159.6 %psum.7 = f32[8,8,1,1,32]{4,1,3,2,0:T(8,128)} all-reduce(f32[8,8,1,1,32]{4,1,3,2,0:T(8,128)S(1)} %stack.11), channel_id=1, replica_groups=mesh['slab'=128,'rep'=4] {'rep'}, use_global_device_ids=true, to_apply=%region_1.2 | all-reduce | flops 2048 | bytes 16384 | tf_op jit(solution)/shard_map/psum | solution.py:145
  1604.3 3.4 fusion.11
  1607.8 1.3 maximum_bitcast_fusion.4
  (14 shorter events, 0.3 us)
Async XLA Ops:
  7.2 1151.9 %all-reduce.3.cloned.1.call-start = ((), (), s32[]{:S(2)}) async-start(), calls=%async_computation | async-start | bytes 12582912
  27.4 0.7 copy-start.1
  30.1 4.5 copy-start
Sparse Core Ops, SparseCore 0:
  27.6 1131.3 all-reduce.2
where the time goes:
time: 1620 us
  waiting for transfers between devices  1110 us (69%)
  blocking collectives  426 us (26%)
  matrix products  24 us (1%)
  other arithmetic  19 us (1%)
  between operations  17 us (1%)
  local copies, waits for them, and re-layouts  16.6 us (1%)
    unnamed x2, waiting for transfers between devices  1110 us
    all_gather x1, blocking collectives, shards(): lax.all_gather(mode_grads, 'slab', axis=0, tiled=True)  267 us
    psum x1, blocking collectives, shards(): weight_grad = lax.psum(local_grad, 'rep')  160 us
  transfers between devices with their start and end apart: 1, of which 1 were waited for; matrix products, arithmetic and copies ran while one was open for 1% of the time, Pallas kernels for 0%

commit v1 on v0

v1 whole, which is shorter than its diff:
```python
import functools

import jax
import jax.numpy as jnp
import ml_dtypes
import numpy as np
from jax import lax
from jax.experimental import pallas as pl
from jax.experimental.pallas import tpu as pltpu
from jax.sharding import PartitionSpec as P

N = 256
KM = 32
PLANES = 2
SLABS = 128
GROUPS = 4
SCALE = 2.0**-12
VMEM = pltpu.VMEM


def frequencies():
    counter = np.arange(KM)
    return np.where(counter < KM // 2, counter, counter - KM)


def circle(positions):
    angles = 2.0 * np.pi * ((positions[:, None] * frequencies()[None, :]) % N) / N
    return np.cos(angles), np.sin(angles)


def split(table):
    high = table.astype(ml_dtypes.bfloat16)
    low = (table - high.astype(np.float64)).astype(ml_dtypes.bfloat16)
    return high, low


def interleave(real, imag):
    rows = real.shape[0]
    both = np.stack([real.reshape(rows, GROUPS, 8), imag.reshape(rows, GROUPS, 8)], axis=2)
    return both.reshape(rows, 2 * KM)


@functools.cache
def tables():
    cos, sin = circle(np.arange(N))
    from_real = np.concatenate(split(interleave(cos, -sin)), axis=1)
    from_imag = np.concatenate(split(interleave(sin, cos)), axis=1)
    forward_y = np.stack([from_real, from_imag])
    forward_x = np.concatenate(split(np.concatenate([cos.T, sin.T], axis=0)), axis=0)
    depth = np.concatenate([cos, sin], axis=1).astype(np.float32) * np.float32(SCALE)
    depth_back = np.concatenate([depth[0::2], depth[1::2]], axis=1)
    to_real = interleave(cos, -sin).T
    to_imag = interleave(sin, cos).T
    high, low = split(np.concatenate([to_real, to_imag], axis=1))
    inverse_y = np.concatenate([high, high, low, np.zeros_like(low)], axis=0)
    high, low = split(np.block([[cos, -sin], [sin, cos]]))
    inverse_x = np.concatenate([high, high, low], axis=1)
    return forward_y, forward_x, depth, depth_back, inverse_y, inverse_x


def dot(left, right):
    return jnp.dot(left, right, preferred_element_type=jnp.float32)


def exact_dot(left, right, dims):
    return lax.dot_general(
        left,
        right,
        (dims, ((), ())),
        precision=lax.Precision.HIGHEST,
        preferred_element_type=jnp.float32,
    )


def lanes(rows):
    return lax.broadcasted_iota(jnp.int32, (rows, 128), 1)


def roll(value, shift):
    shift = shift % 128
    return value if shift == 0 else pltpu.roll(value, shift, 1)


def forward_kernel(saved_ref, grad_ref, table_y_ref, table_x_ref, out_ref):
    plane = pl.program_id(0)
    low_half = lanes(N) < 64
    is_real = (lanes(KM) // 8) % 2 == 0
    slot = lanes(KM) // 16
    modes = []
    for ref in (saved_ref, grad_ref):
        for axis in range(3):
            rows = dot(ref[axis, 0], table_y_ref[0]) + dot(ref[3 + axis, 0], table_y_ref[1])
            rows = rows + roll(rows, 64)
            high = rows.astype(jnp.bfloat16).astype(jnp.float32)
            rows = jnp.where(low_half, high, rows - high).astype(jnp.bfloat16)
            both = dot(table_x_ref[...], rows)
            both = both[:64] + both[64:]
            both = both + roll(both, 64)
            with_cos, with_sin = both[:KM], both[KM:]
            modes.append(with_cos + jnp.where(is_real, roll(with_sin, -8), -roll(with_sin, 8)))
    for group in range(GROUPS):
        gathered = jnp.zeros((KM, 128), jnp.float32)
        for place, value in enumerate(modes):
            gathered = jnp.where(slot == place, roll(value, 16 * (place - group)), gathered)
        out_ref[pl.ds(group * PLANES + plane, KM, stride=GROUPS * PLANES), :] = gathered


def cross_three(left, right):
    return (
        left[1] * right[2] - left[2] * right[1],
        left[2] * right[0] - left[0] * right[2],
        left[0] * right[1] - left[1] * right[0],
    )


def cross_conjugated(left_real, left_imag, right_real, right_imag):
    first = cross_three(left_real, right_real)
    second = cross_three(left_imag, right_imag)
    third = cross_three(left_real, right_imag)
    fourth = cross_three(left_imag, right_real)
    return [a + b for a, b in zip(first, second)], [a - b for a, b in zip(third, fourth)]


def adjoint_product(scalar_real, scalar_imag, vector_real, vector_imag, grad_real, grad_imag):
    cross_real, cross_imag = cross_conjugated(vector_real, vector_imag, grad_real, grad_imag)
    real_part = [
        scalar_real * grad_real[i] + scalar_imag * grad_imag[i] - cross_imag[i] for i in range(3)
    ]
    imag_part = [
        scalar_real * grad_imag[i] - scalar_imag * grad_real[i] + cross_real[i] for i in range(3)
    ]
    return real_part, imag_part


def middle_kernel(planes_ref, weight_ref, depth_ref, back_ref, grad_out_ref, out_ref):
    spectra = exact_dot(planes_ref[...].T, depth_ref[...], ((1,), (0,)))
    with_cos, with_sin = spectra[:, :KM], spectra[:, KM:]
    real, imag = [], []
    for place in range(6):
        at_real, at_imag = slice(16 * place, 16 * place + 8), slice(16 * place + 8, 16 * place + 16)
        real.append(with_cos[at_real] + with_sin[at_imag])
        imag.append(with_cos[at_imag] - with_sin[at_real])
    inputs_real, inputs_imag, grads_real, grads_imag = real[:3], imag[:3], real[3:], imag[3:]
    scalar_real = sum(
        inputs_real[i] * grads_real[i] + inputs_imag[i] * grads_imag[i] for i in range(3)
    )
    scalar_imag = sum(
        inputs_real[i] * grads_imag[i] - inputs_imag[i] * grads_real[i] for i in range(3)
    )
    cross_real, cross_imag = cross_conjugated(inputs_real, inputs_imag, grads_real, grads_imag)
    blades = [scalar_real] + cross_imag + [scalar_imag] + [-entry for entry in cross_real]
    for blade, entry in enumerate(blades):
        grad_out_ref[:, blade, :] = entry
    weight = [weight_ref[:, blade, :] for blade in range(8)]
    mode_real, mode_imag = adjoint_product(
        weight[0], weight[4], weight[1:4], weight[5:8], grads_real, grads_imag
    )
    straight, turned = [], []
    for i in range(3):
        straight += [mode_real[i], mode_imag[i]]
        turned += [-mode_imag[i], mode_real[i]]
    pair = jnp.concatenate(
        [jnp.concatenate(straight, axis=0), jnp.concatenate(turned, axis=0)], axis=1
    )
    pair = jnp.concatenate([pair, jnp.zeros((16, 64), jnp.float32)], axis=0)
    nothing = jnp.zeros((64, 64), jnp.float32)
    blocks = jnp.concatenate(
        [
            jnp.concatenate([pair, nothing], axis=1),
            jnp.concatenate([nothing, pair], axis=1),
        ],
        axis=0,
    )
    out_ref[...] = exact_dot(back_ref[...], blocks, ((1,), (1,)))


def backward_kernel(modes_ref, grad_ref, bypass_ref, table_y_ref, table_x_ref, out_ref, spec_ref):
    plane = pl.program_id(0)
    low_half = lanes(KM) < 64
    slot = lanes(KM) // 16
    groups = []
    for group in range(GROUPS):
        value = modes_ref[pl.ds(group, KM, stride=GROUPS), :]
        groups.append(jnp.where(plane == 0, value, roll(value, 64)))
    left = []
    for axis in range(3):
        gathered = jnp.zeros((KM, 128), jnp.float32)
        for place in range(8):
            gathered = jnp.where(
                slot == place, roll(groups[place % GROUPS], 16 * (place - axis)), gathered
            )
        high = gathered.astype(jnp.bfloat16).astype(jnp.float32)
        first = jnp.where(low_half, high, gathered - high)
        second = jnp.where(low_half, high, 0.0)
        left.append(jnp.concatenate([first, second], axis=1).astype(jnp.bfloat16))
    along_y = dot(jnp.concatenate(left, axis=0), table_y_ref[...])
    for axis in range(3):
        rows = along_y[axis * KM : (axis + 1) * KM]
        rows = jnp.concatenate([rows[:, :N], rows[:, N:]], axis=0)
        high = rows.astype(jnp.bfloat16)
        low = (rows - high.astype(jnp.float32)).astype(jnp.bfloat16)
        spec_ref[axis] = dot(table_x_ref[...], jnp.concatenate([high, low, high], axis=0))
    weight = [bypass_ref[blade] for blade in range(8)]
    step = 16

    def chunk(index, carry):
        start = pl.multiple_of(index * step, step)
        here = pl.ds(start, step)
        fields = [grad_ref[entry, 0, here, :].astype(jnp.float32) for entry in range(6)]
        real, imag = adjoint_product(
            weight[0], weight[4], weight[1:4], weight[5:8], fields[:3], fields[3:]
        )
        for axis in range(3):
            total = spec_ref[axis, here, :] + real[axis]
            out_ref[axis, 0, here, :] = total.astype(jnp.bfloat16)
            there = pl.ds(pl.multiple_of(start + N, step), step)
            total = spec_ref[axis, there, :] + imag[axis]
            out_ref[3 + axis, 0, here, :] = total.astype(jnp.bfloat16)
        return carry

    lax.fori_loop(0, N // step, chunk, 0)


def whole(shape):
    return pl.BlockSpec(shape, lambda *_: (0,) * len(shape))


FIELD = pl.BlockSpec((6, 1, N, N), lambda plane: (0, plane, 0, 0))
PARAMS = pltpu.CompilerParams(vmem_limit_bytes=32 * 1024 * 1024)


def forward(saved, grad, table_y, table_x, interpret=False):
    return pl.pallas_call(
        forward_kernel,
        grid=(PLANES,),
        in_specs=[FIELD, FIELD, whole((2, N, 128)), whole((128, N))],
        out_specs=whole((SLABS * PLANES, 128)),
        out_shape=jax.ShapeDtypeStruct((SLABS * PLANES, 128), jnp.float32),
        compiler_params=PARAMS,
        interpret=interpret,
        name="to_plane_modes",
    )(saved, grad, table_y, table_x)


def middle(planes, weight, depth, back, interpret=False):
    return pl.pallas_call(
        middle_kernel,
        out_shape=(
            jax.ShapeDtypeStruct((8, 8, KM), jnp.float32),
            jax.ShapeDtypeStruct((SLABS, 128), jnp.float32),
        ),
        compiler_params=PARAMS,
        interpret=interpret,
        name="mode_products",
    )(planes, weight, depth, back)


def backward(modes, grad, bypass, table_y, table_x, interpret=False):
    return pl.pallas_call(
        backward_kernel,
        grid=(PLANES,),
        in_specs=[
            whole((SLABS, 128)),
            FIELD,
            pl.BlockSpec(memory_space=pltpu.SMEM),
            whole((N, 2 * N)),
            whole((2 * N, 192)),
        ],
        out_specs=FIELD,
        out_shape=jax.ShapeDtypeStruct((6, PLANES, N, N), jnp.bfloat16),
        scratch_shapes=[VMEM((3, 2 * N, N), jnp.float32)],
        compiler_params=PARAMS,
        interpret=interpret,
        name="to_input_grad",
    )(modes, grad, bypass, table_y, table_x)


def shards(saved_input, output_grad, spectral_weight, bypass_weight):
    forward_y, forward_x, depth, depth_back, inverse_y, inverse_x = tables()
    saved = saved_input.reshape(6, PLANES, N, N)
    grad = output_grad.reshape(6, PLANES, N, N)
    modes = forward(saved, grad, forward_y, forward_x)
    rows = lax.all_to_all(modes.reshape(SLABS, PLANES, 128), "slab", 0, 0, tiled=True)
    local_grad, mode_grads = middle(
        rows.reshape(SLABS * PLANES, 128), spectral_weight.reshape(8, 8, KM), depth, depth_back
    )
    back = lax.all_to_all(mode_grads.reshape(SLABS, 1, 128), "slab", 0, 0, tiled=True)
    weight_grad = jnp.sum(lax.all_gather(local_grad, "rep"), axis=0)
    input_grad = backward(
        back.reshape(SLABS, 128), grad, bypass_weight.reshape(8), inverse_y, inverse_x
    )
    return (
        input_grad.reshape(1, 6, 1, PLANES, N, N),
        weight_grad.reshape(8, 8, 1, 1, KM),
    )


def solution(mesh):
    field = P("rep", None, None, "slab", None, None)
    weight = P("slab", None, None, None, None)
    return jax.shard_map(
        shards,
        mesh=mesh,
        in_specs=(field, field, weight, P()),
        out_specs=(field, weight),
        check_vma=False,
    )
```

time: 1620 us -> 67.3 us (0.04)
  the two profiles are of different devices: /device:TPU:1 before, /device:TPU:4 now
where the time goes in v1:
time: 67.3 us; the launch traced here: 66.9 us
  blocking collectives  38.6 us (57%)
  Pallas kernels  11 us (16%)
  starting transfers between devices  6.15 us (9%)
  waiting for transfers between devices  5.25 us (8%)
  local copies, waits for them, and re-layouts  4.58 us (7%)
  between operations  0.71 us (1%)
    all_to_all x1, blocking collectives, shards(): lax.all_to_all(modes.reshape(SLABS, PLANES, 128), 'slab', 0, 0, tiled=True)  31.6 us
    all_gather x1, blocking collectives, shards(): weight_grad = jnp.sum(lax.all_gather(local_grad, 'rep'), axis=0)  6.96 us
    all_to_all x1, starting transfers between devices, shards(): lax.all_to_all(mode_grads.reshape(SLABS, 1, 128), 'slab', 0, 0, tiled=True)  6.15 us
    all_to_all x1, waiting for transfers between devices, shards(): lax.all_to_all(mode_grads.reshape(SLABS, 1, 128), 'slab', 0, 0, tiled=True)  5.25 us
    pallas_call x1, Pallas kernels, forward(): pl.pallas_call(forward_kernel, grid=(PLANES,), in_specs=[FIELD, FIELD, wh...  5.14 us
    unnamed x22, local copies, waits for them, and re-layouts  4.58 us
    pallas_call x1, Pallas kernels, backward(): pl.pallas_call(backward_kernel, grid=(PLANES,), in_specs=[whole((SLABS, 1...  4.39 us
    pallas_call x1, Pallas kernels, middle(): pl.pallas_call(middle_kernel, out_shape=(jax.ShapeDtypeStruct((8, 8, KM),...  1.52 us
  transfers between devices with their start and end apart: 1, of which 1 were waited for; matrix products, arithmetic and copies ran while one was open for 1% of the time, Pallas kernels for 0%

profile of v1, /device:TPU:4, one launch (start us, length us, event | category | flops | bytes accessed | tf_op | source)
XLA Modules:
  0.0 66.9 jit_solution(10045346518627374569)
XLA Ops:
  0.6 0.0 copy-start
  0.6 1.4 %copy-done = bf16[1,6,1,2,256,256]{5,4,3,2,1,0:T(8,128)(2,1)S(1)} copy-done((bf16[1,6,1,2,256,256]{5,4,3,2,1,0:T(8,128)(2,1)S(1)}, bf16[1,6,1,2,256,256]{5,4,3,2,1,0:T(8,128)(2,1)}, u32[]{:S(2)}) %copy-start) | copy-done | bytes 1572888
  2.0 0.0 copy-start.2
  2.0 1.4 %copy-done.2 = bf16[1,6,1,2,256,256]{5,4,3,2,1,0:T(8,128)(2,1)S(1)} copy-done((bf16[1,6,1,2,256,256]{5,4,3,2,1,0:T(8,128)(2,1)S(1)}, bf16[1,6,1,2,256,256]{5,4,3,2,1,0:T(8,128)(2,1)}, u32[]{:S(2)}) %copy-start.2) | copy-done | bytes 1572888
  3.4 0.0 copy-start.6
  3.5 0.9 %copy-done.6 = bf16[2,256,128]{2,1,0:T(8,128)(2,1)S(1)} copy-done((bf16[2,256,128]{2,1,0:T(8,128)(2,1)S(1)}, bf16[2,256,128]{2,1,0:T(8,128)(2,1)}, u32[]{:S(2)}) %copy-start.6) | copy-done | bytes 131096
  4.4 0.0 copy-start.7
  4.4 0.8 %copy-done.7 = bf16[128,256]{1,0:T(8,128)(2,1)S(1)} copy-done((bf16[128,256]{1,0:T(8,128)(2,1)S(1)}, bf16[128,256]{1,0:T(8,128)(2,1)}, u32[]{:S(2)}) %copy-start.7) | copy-done | bytes 65560
  5.2 0.0 copy-start.5
  5.2 0.0 copy-start.8
  5.2 0.0 copy-start.9
  5.2 0.0 copy-start.1
  5.2 0.0 copy-start.3
  5.2 0.0 copy-start.4
  5.2 0.0 copy-start.10
  5.2 5.1 %to_plane_modes.1 = f32[256,128]{1,0:T(8,128)S(1)} custom-call(bf16[6,2,256,256]{3,2,1,0:T(8,128)(2,1)S(1)} %bitcast.17, bf16[6,2,256,256]{3,2,1,0:T(8,128)(2,1)S(1)} %bitcast.15, bf16[2,256,128]{2,1,0:T(8,128)(2,1)S(1)} %copy-done.6, bf16[128,256]{1,0:T(8,128)(2,1)S(1)} %copy-done.7), custom_call_target="tpu_custom_call" | custom-call | tf_op jit(solution)/shard_map/to_plane_modes/pallas_call | solution.py:233
  10.4 31.6 %all_to_all.10 = f32[128,2,128]{2,1,0:T(2,128)S(1)} all-to-all(f32[128,2,128]{2,1,0:T(2,128)S(1)} %bitcast.19), channel_id=1, replica_groups=mesh['slab'=128,'rep'=4] {'slab'}, dimensions={0} | all-to-all | bytes 262144 | tf_op jit(solution)/shard_map/all_to_all | solution.py:283
  42.0 0.0 copy-done.5
  42.0 0.0 copy-done.8
  42.0 0.0 copy-done.9
  42.0 1.5 %mode_products.1 = (f32[8,8,32]{2,1,0:T(8,128)S(1)}, f32[128,128]{1,0:T(8,128)}) custom-call(f32[256,128]{1,0:T(8,128)S(1)} %bitcast.18, f32[8,8,32]{2,1,0:T(8,128)S(1)} %bitcast.21, f32[256,64]{1,0:T(8,128)S(1)} %copy-done.5, f32[128,128]{1,0:T(8,128)S(1)} %copy-done.8), custom_call_target="tpu_custom_call" | custom-call | tf_op jit(solution)/shard_map/mode_products/pallas_call | solution.py:246
  43.5 6.1 %all-to-all-start.1 = ((f32[128,1,128]{2,1,0:T(1,128)}), f32[128,1,128]{2,1,0:T(1,128)S(1)}, u32[]{:S(2)}, u32[]{:S(2)}) async-start(f32[128,1,128]{2,1,0:T(1,128)} %bitcast.6), calls=%async_computation.1 | async-start | bytes 131072 | tf_op jit(solution)/shard_map/all_to_all | solution.py:287
  49.7 7.0 %all-gather = f32[32,8,32]{2,1,0:T(8,128)S(1)} all-gather(f32[8,8,32]{2,1,0:T(8,128)S(1)} %get-tuple-element.5), channel_id=2, replica_groups=mesh['slab'=128,'rep'=4] {'rep'}, dimensions={0}, use_global_device_ids=true | all-gather | bytes 40960 | tf_op jit(solution)/shard_map/all_gather | solution.py:288
  56.7 0.6 reduce_sum.9
  57.3 5.3 %all-to-all-done.1 = f32[128,1,128]{2,1,0:T(1,128)S(1)} async-done(((f32[128,1,128]{2,1,0:T(1,128)}), f32[128,1,128]{2,1,0:T(1,128)S(1)}, u32[]{:S(2)}, u32[]{:S(2)}) %all-to-all-start.1) | async-done | bytes 65568 | tf_op jit(solution)/shard_map/all_to_all | solution.py:287
  62.5 0.0 copy-done.1
  62.5 0.0 copy-done.3
  62.5 0.0 copy-done.4
  62.5 0.0 copy-done.10
  62.6 4.4 %to_input_grad.1 = bf16[6,2,256,256]{3,2,1,0:T(8,128)(2,1)} custom-call(f32[128,128]{1,0:T(8,128)S(1)} %bitcast.20, bf16[6,2,256,256]{3,2,1,0:T(8,128)(2,1)S(1)} %bitcast.16, f32[8]{0:T(128)S(1)} %bitcast.22, bf16[256,512]{1,0:T(8,128)(2,1)S(1)} %copy-done.4, bf16[512,192]{1,0:T(8,128)(2,1)S(1)} %copy-done.3), custom_call_target="tpu_custom_call" | custom-call | tf_op jit(solution)/shard_map/to_input_grad/pallas_call | solution.py:259
Async XLA Ops:
  0.6 1.4 %copy-start = (bf16[1,6,1,2,256,256]{5,4,3,2,1,0:T(8,128)(2,1)S(1)}, bf16[1,6,1,2,256,256]{5,4,3,2,1,0:T(8,128)(2,1)}, u32[]{:S(2)}) copy-start(bf16[1,6,1,2,256,256]{5,4,3,2,1,0:T(8,128)(2,1)} %param.11) | copy-start | bytes 4718596
  2.0 1.4 %copy-start.2 = (bf16[1,6,1,2,256,256]{5,4,3,2,1,0:T(8,128)(2,1)S(1)}, bf16[1,6,1,2,256,256]{5,4,3,2,1,0:T(8,128)(2,1)}, u32[]{:S(2)}) copy-start(bf16[1,6,1,2,256,256]{5,4,3,2,1,0:T(8,128)(2,1)} %param.10) | copy-start | bytes 4718596
  3.4 0.9 %copy-start.6 = (bf16[2,256,128]{2,1,0:T(8,128)(2,1)S(1)}, bf16[2,256,128]{2,1,0:T(8,128)(2,1)}, u32[]{:S(2)}) copy-start(bf16[2,256,128]{2,1,0:T(8,128)(2,1)} %constant.14.clone.table_y_ref) | copy-start | bytes 393220
  4.4 0.8 %copy-start.7 = (bf16[128,256]{1,0:T(8,128)(2,1)S(1)}, bf16[128,256]{1,0:T(8,128)(2,1)}, u32[]{:S(2)}) copy-start(bf16[128,256]{1,0:T(8,128)(2,1)} %constant.15.clone.table_x_ref) | copy-start | bytes 196612
  5.2 36.8 %copy-start.5 = (f32[256,64]{1,0:T(8,128)S(1)}, f32[256,64]{1,0:T(8,128)}, u32[]{:S(2)}) copy-start(f32[256,64]{1,0:T(8,128)} %constant.16.clone.depth_ref) | copy-start | bytes 196612
  5.2 36.8 %copy-start.8 = (f32[128,128]{1,0:T(8,128)S(1)}, f32[128,128]{1,0:T(8,128)}, u32[]{:S(2)}) copy-start(f32[128,128]{1,0:T(8,128)} %constant.17.clone.back_ref) | copy-start | bytes 196612
  5.2 36.8 %copy-start.9 = (f32[8,8,1,1,32]{4,3,2,1,0:T(1,128)S(1)}, f32[8,8,1,1,32]{4,3,2,1,0:T(1,128)}, u32[]{:S(2)}) copy-start(f32[8,8,1,1,32]{4,3,2,1,0:T(1,128)} %param.12) | copy-start | bytes 24580
  5.2 57.3 %copy-start.1 = (bf16[1,6,1,2,256,256]{5,4,3,2,1,0:T(8,128)(2,1)S(1)}, bf16[1,6,1,2,256,256]{5,4,3,2,1,0:T(8,128)(2,1)}, u32[]{:S(2)}) copy-start(bf16[1,6,1,2,256,256]{5,4,3,2,1,0:T(8,128)(2,1)} %param.11) | copy-start | bytes 4718596
  5.2 57.3 %copy-start.3 = (bf16[512,192]{1,0:T(8,128)(2,1)S(1)}, bf16[512,192]{1,0:T(8,128)(2,1)}, u32[]{:S(2)}) copy-start(bf16[512,192]{1,0:T(8,128)(2,1)} %constant.19.clone.table_x_ref) | copy-start | bytes 589828
  5.2 57.3 %copy-start.4 = (bf16[256,512]{1,0:T(8,128)(2,1)S(1)}, bf16[256,512]{1,0:T(8,128)(2,1)}, u32[]{:S(2)}) copy-start(bf16[256,512]{1,0:T(8,128)(2,1)} %constant.18.clone.table_y_ref) | copy-start | bytes 786436
  5.2 57.3 %copy-start.10 = (f32[8,1,1]{0,2,1:T(1,128)S(1)}, f32[8,1,1]{0,2,1:T(1,128)}, u32[]{:S(2)}) copy-start(f32[8,1,1]{0,2,1:T(1,128)} %param.13) | copy-start | bytes 100
  43.5 19.0 %all-to-all-start.1 = ((f32[128,1,128]{2,1,0:T(1,128)}), f32[128,1,128]{2,1,0:T(1,128)S(1)}, u32[]{:S(2)}, u32[]{:S(2)}) async-start(f32[128,1,128]{2,1,0:T(1,128)} %bitcast.6), calls=%async_computation.1 | async-start | bytes 131072 | tf_op jit(solution)/shard_map/all_to_all | solution.py:287

commit v2 on v1

v2 whole, which is shorter than its diff:
```python
import functools

import jax
import jax.numpy as jnp
import ml_dtypes
import numpy as np
from jax import lax
from jax.experimental import pallas as pl
from jax.experimental.pallas import tpu as pltpu
from jax.sharding import PartitionSpec as P

N = 256
KM = 32
PLANES = 2
SLABS = 128
GROUPS = 4
SCALE = 2.0**-12


def frequencies():
    counter = np.arange(KM)
    return np.where(counter < KM // 2, counter, counter - KM)


def circle(positions):
    angles = 2.0 * np.pi * ((positions[:, None] * frequencies()[None, :]) % N) / N
    return np.cos(angles), np.sin(angles)


def split(table):
    high = table.astype(ml_dtypes.bfloat16)
    low = (table - high.astype(np.float64)).astype(ml_dtypes.bfloat16)
    return high, low


def interleave(real, imag):
    rows = real.shape[0]
    both = np.stack([real.reshape(rows, GROUPS, 8), imag.reshape(rows, GROUPS, 8)], axis=2)
    return both.reshape(rows, 2 * KM)


@functools.cache
def tables():
    cos, sin = circle(np.arange(N))
    from_real = np.concatenate(split(interleave(cos, -sin)), axis=1)
    from_imag = np.concatenate(split(interleave(sin, cos)), axis=1)
    forward_y = np.stack([from_real, from_imag])
    forward_x = np.concatenate(split(np.concatenate([cos.T, sin.T], axis=0)), axis=0)
    depth = np.concatenate([cos, sin], axis=1) * SCALE
    high, low = split(np.concatenate([depth[0::2], depth[1::2]], axis=1))
    depth_back = np.concatenate([high, high, low], axis=1)
    depth = np.concatenate(split(depth), axis=1)
    to_real = interleave(cos, -sin).T
    to_imag = interleave(sin, cos).T
    high, low = split(np.concatenate([to_real, to_imag], axis=1))
    inverse_y = np.concatenate([high, high, low, np.zeros_like(low)], axis=0)
    high, low = split(np.block([[cos, -sin], [sin, cos]]))
    inverse_x = np.concatenate([high, high, low], axis=1)
    return forward_y, forward_x, depth, depth_back, inverse_y, inverse_x


def dot(left, right):
    return jnp.dot(left, right, preferred_element_type=jnp.float32)


def lanes(rows):
    return lax.broadcasted_iota(jnp.int32, (rows, 128), 1)


def roll(value, shift):
    shift = shift % 128
    return value if shift == 0 else pltpu.roll(value, shift, 1)


def forward_kernel(saved_ref, grad_ref, far_y_ref, far_x_ref, out_ref, fields, table_y, table_x, rows_ref, sems):
    copies = [
        pltpu.make_async_copy(far_y_ref, table_y, sems.at[0]),
        pltpu.make_async_copy(far_x_ref, table_x, sems.at[1]),
    ]
    for field, ref in enumerate((saved_ref, grad_ref)):
        for entry in range(6):
            copies.append(
                pltpu.make_async_copy(
                    ref.at[entry], fields.at[field, entry], sems.at[2 + 6 * field + entry]
                )
            )
    for copy in copies:
        copy.start()
    for copy in copies:
        copy.wait()
    is_real = (lanes(KM) // 8) % 2 == 0
    slot = lanes(KM) // 16
    places = [(field, axis) for field in range(2) for axis in range(3)]
    for place, (field, axis) in enumerate(places):
        real = fields[field, axis].reshape(PLANES * N, N)
        imag = fields[field, 3 + axis].reshape(PLANES * N, N)
        rows = dot(real, table_y[0]) + dot(imag, table_y[1])
        high = rows.astype(jnp.bfloat16)
        rows_ref[place, :, :128] = high
        rows_ref[place, :, 128:] = (rows - high.astype(jnp.float32)).astype(jnp.bfloat16)
    for plane in range(PLANES):
        modes = []
        for place in range(6):
            both = dot(table_x[...], rows_ref[place, plane * N : (plane + 1) * N, :])
            both = both[:64] + both[64:]
            both = both[:, :128] + both[:, 128:]
            both = both + roll(both, 64)
            with_cos, with_sin = both[:KM], both[KM:]
            modes.append(with_cos + jnp.where(is_real, roll(with_sin, -8), -roll(with_sin, 8)))
        for group in range(GROUPS):
            gathered = jnp.zeros((KM, 128), jnp.float32)
            for place, value in enumerate(modes):
                gathered = jnp.where(slot == place, roll(value, 16 * (place - group)), gathered)
            out_ref[pl.ds(group * PLANES + plane, KM, stride=GROUPS * PLANES), :] = gathered


def cross_three(left, right):
    return (
        left[1] * right[2] - left[2] * right[1],
        left[2] * right[0] - left[0] * right[2],
        left[0] * right[1] - left[1] * right[0],
    )


def cross_conjugated(left_real, left_imag, right_real, right_imag):
    first = cross_three(left_real, right_real)
    second = cross_three(left_imag, right_imag)
    third = cross_three(left_real, right_imag)
    fourth = cross_three(left_imag, right_real)
    return [a + b for a, b in zip(first, second)], [a - b for a, b in zip(third, fourth)]


def adjoint_product(scalar_real, scalar_imag, vector_real, vector_imag, grad_real, grad_imag):
    cross_real, cross_imag = cross_conjugated(vector_real, vector_imag, grad_real, grad_imag)
    real_part = [
        scalar_real * grad_real[i] + scalar_imag * grad_imag[i] - cross_imag[i] for i in range(3)
    ]
    imag_part = [
        scalar_real * grad_imag[i] - scalar_imag * grad_real[i] + cross_real[i] for i in range(3)
    ]
    return real_part, imag_part


def middle_kernel(planes_ref, weight_ref, depth_ref, back_ref, grad_out_ref, out_ref):
    planes = planes_ref[...].T
    high = planes.astype(jnp.bfloat16)
    low = (planes - high.astype(jnp.float32)).astype(jnp.bfloat16)
    spectra = dot(high, depth_ref[...]) + dot(low, depth_ref[...])
    spectra = spectra + roll(spectra, 64)
    with_cos, with_sin = spectra[:, :KM], spectra[:, KM:64]
    real, imag = [], []
    for place in range(6):
        at_real, at_imag = slice(16 * place, 16 * place + 8), slice(16 * place + 8, 16 * place + 16)
        real.append(with_cos[at_real] + with_sin[at_imag])
        imag.append(with_cos[at_imag] - with_sin[at_real])
    inputs_real, inputs_imag, grads_real, grads_imag = real[:3], imag[:3], real[3:], imag[3:]
    scalar_real = sum(
        inputs_real[i] * grads_real[i] + inputs_imag[i] * grads_imag[i] for i in range(3)
    )
    scalar_imag = sum(
        inputs_real[i] * grads_imag[i] - inputs_imag[i] * grads_real[i] for i in range(3)
    )
    cross_real, cross_imag = cross_conjugated(inputs_real, inputs_imag, grads_real, grads_imag)
    blades = [scalar_real] + cross_imag + [scalar_imag] + [-entry for entry in cross_real]
    for blade, entry in enumerate(blades):
        grad_out_ref[:, blade, :] = entry
    weight = [weight_ref[:, blade, :] for blade in range(8)]
    mode_real, mode_imag = adjoint_product(
        weight[0], weight[4], weight[1:4], weight[5:8], grads_real, grads_imag
    )
    straight, turned = [], []
    for i in range(3):
        straight += [mode_real[i], mode_imag[i]]
        turned += [-mode_imag[i], mode_real[i]]
    pair = jnp.concatenate(
        [jnp.concatenate(straight, axis=0), jnp.concatenate(turned, axis=0)], axis=1
    )
    pair = jnp.concatenate([pair, jnp.zeros((16, 64), jnp.float32)], axis=0)
    nothing = jnp.zeros((64, 64), jnp.float32)
    blocks = jnp.concatenate(
        [
            jnp.concatenate([pair, nothing], axis=1),
            jnp.concatenate([nothing, pair], axis=1),
        ],
        axis=0,
    )
    high = blocks.astype(jnp.bfloat16)
    low = (blocks - high.astype(jnp.float32)).astype(jnp.bfloat16)
    out_ref[...] = lax.dot_general(
        back_ref[...],
        jnp.concatenate([high, low, high], axis=1),
        (((1,), (1,)), ((), ())),
        preferred_element_type=jnp.float32,
    )


def bypass_kernel(grad_ref, bypass_ref, out_ref, field, sems):
    copies = [
        pltpu.make_async_copy(grad_ref.at[:, plane], field.at[:, plane], sems.at[plane])
        for plane in range(PLANES)
    ]
    for copy in copies:
        copy.start()
    weight = [bypass_ref[blade] for blade in range(8)]
    step = 32
    for plane in range(PLANES):
        copies[plane].wait()

        def chunk(index, carry):
            here = pl.ds(pl.multiple_of(index * step, step), step)
            fields = [field[entry, plane, here, :].astype(jnp.float32) for entry in range(6)]
            real, imag = adjoint_product(
                weight[0], weight[4], weight[1:4], weight[5:8], fields[:3], fields[3:]
            )
            for axis in range(3):
                out_ref[axis, plane, here, :] = real[axis]
                out_ref[3 + axis, plane, here, :] = imag[axis]
            return carry

        lax.fori_loop(0, N // step, chunk, 0)

def backward_kernel(
    modes_ref, bypass_ref, far_y_ref, far_x_ref, out_ref, table_y, table_x, total_ref, near_sems, sems
):
    fetch_y = pltpu.make_async_copy(far_y_ref, table_y, near_sems.at[0])
    fetch_x = pltpu.make_async_copy(far_x_ref, table_x, near_sems.at[1])
    fetch_y.start()
    fetch_x.start()
    low_half = lanes(KM) < 64
    slot = lanes(KM) // 16
    groups = [modes_ref[pl.ds(group, KM, stride=GROUPS), :] for group in range(GROUPS)]
    left = []
    for plane in range(PLANES):
        for axis in range(3):
            gathered = jnp.zeros((KM, 128), jnp.float32)
            for place in range(8):
                value = roll(groups[place % GROUPS], 16 * (place - axis) - 64 * plane)
                gathered = jnp.where(slot == place, value, gathered)
            high = gathered.astype(jnp.bfloat16).astype(jnp.float32)
            first = jnp.where(low_half, high, gathered - high)
            second = jnp.where(low_half, high, 0.0)
            left.append(jnp.concatenate([first, second], axis=1).astype(jnp.bfloat16))
    left = jnp.concatenate(left, axis=0)
    fetch_y.wait()
    fetch_x.wait()
    along_y = dot(left, table_y[...])
    right = []
    for part in range(3 * PLANES):
        rows = along_y[part * KM : (part + 1) * KM]
        rows = jnp.concatenate([rows[:, :N], rows[:, N:]], axis=0)
        high = rows.astype(jnp.bfloat16)
        low = (rows - high.astype(jnp.float32)).astype(jnp.bfloat16)
        right.append(jnp.concatenate([high, low, high], axis=0))
    copies = []
    for part in range(3 * PLANES):
        plane, axis = divmod(part, 3)
        spectral = dot(table_x[...], right[part])
        for entry, rows in ((axis, spectral[:N]), (3 + axis, spectral[N:])):
            total = rows + bypass_ref[entry, plane]
            total_ref[entry, plane] = total.astype(jnp.bfloat16)
        for entry in (axis, 3 + axis):
            copies.append(
                pltpu.make_async_copy(
                    total_ref.at[entry, plane], out_ref.at[entry, plane], sems.at[entry, plane]
                )
            )
            copies[-1].start()
    for copy in copies:
        copy.wait()


NEAR = pl.BlockSpec(memory_space=pltpu.VMEM)
FAR = pl.BlockSpec(memory_space=pltpu.HBM)


def params(mebibytes):
    return pltpu.CompilerParams(vmem_limit_bytes=mebibytes * 1024 * 1024)


def cost(flops, moved):
    return pl.CostEstimate(flops=flops, bytes_accessed=moved, transcendentals=0)


def forward(saved, grad, table_y, table_x, interpret=False):
    return pl.pallas_call(
        forward_kernel,
        in_specs=[FAR] * 4,
        out_specs=NEAR,
        out_shape=jax.ShapeDtypeStruct((SLABS * PLANES, 128), jnp.float32),
        scratch_shapes=[
            pltpu.VMEM((2, 6, PLANES, N, N), jnp.bfloat16),
            pltpu.VMEM((2, N, 128), jnp.bfloat16),
            pltpu.VMEM((128, N), jnp.bfloat16),
            pltpu.VMEM((6, PLANES * N, N), jnp.bfloat16),
            pltpu.SemaphoreType.DMA((14,)),
        ],
        compiler_params=params(24),
        cost_estimate=cost(10**9, 3 * 2**20),
        interpret=interpret,
        name="to_plane_modes",
    )(saved, grad, table_y, table_x)


def middle(planes, weight, depth, back, interpret=False):
    return pl.pallas_call(
        middle_kernel,
        in_specs=[NEAR] * 4,
        out_specs=(NEAR, NEAR),
        out_shape=(
            jax.ShapeDtypeStruct((8, 8, KM), jnp.float32),
            jax.ShapeDtypeStruct((SLABS, 128), jnp.float32),
        ),
        compiler_params=params(16),
        cost_estimate=cost(10**8, 2**20),
        interpret=interpret,
        name="mode_products",
    )(planes, weight, depth, back)


def bypass(grad, weight, interpret=False):
    return pl.pallas_call(
        bypass_kernel,
        in_specs=[FAR, pl.BlockSpec(memory_space=pltpu.SMEM)],
        out_specs=NEAR,
        out_shape=jax.ShapeDtypeStruct((6, PLANES, N, N), jnp.float32),
        scratch_shapes=[
            pltpu.VMEM((6, PLANES, N, N), jnp.bfloat16),
            pltpu.SemaphoreType.DMA((PLANES,)),
        ],
        compiler_params=params(16),
        cost_estimate=cost(10**8, 6 * 2**20),
        interpret=interpret,
        name="bypass",
    )(grad, weight)


def backward(modes, bypassed, table_y, table_x, interpret=False):
    return pl.pallas_call(
        backward_kernel,
        in_specs=[NEAR, NEAR, FAR, FAR],
        out_specs=FAR,
        out_shape=jax.ShapeDtypeStruct((6, PLANES, N, N), jnp.bfloat16),
        scratch_shapes=[
            pltpu.VMEM((N, 2 * N), jnp.bfloat16),
            pltpu.VMEM((2 * N, 192), jnp.bfloat16),
            pltpu.VMEM((6, PLANES, N, N), jnp.bfloat16),
            pltpu.SemaphoreType.DMA((2,)),
            pltpu.SemaphoreType.DMA((6, PLANES)),
        ],
        compiler_params=params(24),
        cost_estimate=cost(10**9, 6 * 2**20),
        interpret=interpret,
        name="to_input_grad",
    )(modes, bypassed, table_y, table_x)


def shards(saved_input, output_grad, spectral_weight, bypass_weight):
    forward_y, forward_x, depth, depth_back, inverse_y, inverse_x = tables()
    saved = saved_input.reshape(6, PLANES, N, N)
    grad = output_grad.reshape(6, PLANES, N, N)
    far = functools.partial(pltpu.with_memory_space_constraint, memory_space=pltpu.HBM)
    modes = forward(far(saved), far(grad), far(forward_y), far(forward_x))
    rows = lax.all_to_all(modes.reshape(SLABS, PLANES, 128), "slab", 0, 0, tiled=True)
    local_grad, mode_grads = middle(
        rows.reshape(SLABS * PLANES, 128), spectral_weight.reshape(8, 8, KM), depth, depth_back
    )
    back = lax.all_to_all(mode_grads.reshape(SLABS, 1, 128), "slab", 0, 0, tiled=True)
    local_grad, later = lax.optimization_barrier((local_grad, grad))
    bypassed = bypass(far(later), bypass_weight.reshape(8))
    weight_grad = jnp.sum(lax.all_gather(local_grad, "rep"), axis=0)
    input_grad = backward(back.reshape(SLABS, 128), bypassed, far(inverse_y), far(inverse_x))
    return (
        input_grad.reshape(1, 6, 1, PLANES, N, N),
        weight_grad.reshape(8, 8, 1, 1, KM),
    )


def solution(mesh):
    field = P("rep", None, None, "slab", None, None)
    weight = P("slab", None, None, None, None)
    return jax.shard_map(
        shards,
        mesh=mesh,
        in_specs=(field, field, weight, P()),
        out_specs=(field, weight),
        check_vma=False,
    )
```

time: 67.3 us -> 59.3 us (0.88)
  local copies, waits for them, and re-layouts: 4.58 us -> 0.02 us
  waiting for transfers between devices: 5.25 us -> 2.27 us
    unnamed x22 -> x8, local copies, waits for them, and re-layouts: 4.58 us -> 0.02 us
    all_to_all x1, waiting for transfers between devices: 5.25 us -> 2.27 us  [shards(): lax.all_to_all(mode_grads.reshape(SLABS, 1, 128), 'slab', 0, 0, tiled=True)]
    pallas_call x3 -> x4, Pallas kernels: 11 us -> 10.7 us  [the longest x1 3.58 us: forward(): pl.pallas_call(forward_kernel, in_specs=[FAR] * 4, out_specs=NEAR, out_sh...]
  transfers between devices with their start and end apart: 1 -> 1, of which waited for: 1 -> 1; matrix products, arithmetic and copies ran while one was open for 1% -> 1% of each run, Pallas kernels for 0% -> 5%
where the time goes in v2:
time: 59.3 us; the launch traced here: 59 us
  blocking collectives  38.6 us (65%)
  Pallas kernels  10.7 us (18%)
  starting transfers between devices  6.15 us (10%)
  waiting for transfers between devices  2.27 us (4%)
  between operations  0.69 us (1%)
  other arithmetic  0.63 us (1%)
    all_to_all x1, blocking collectives, shards(): lax.all_to_all(modes.reshape(SLABS, PLANES, 128), 'slab', 0, 0, tiled=True)  31.6 us
    all_gather x1, blocking collectives, shards(): weight_grad = jnp.sum(lax.all_gather(local_grad, 'rep'), axis=0)  6.96 us
    all_to_all x1, starting transfers between devices, shards(): lax.all_to_all(mode_grads.reshape(SLABS, 1, 128), 'slab', 0, 0, tiled=True)  6.15 us
    pallas_call x1, Pallas kernels, forward(): pl.pallas_call(forward_kernel, in_specs=[FAR] * 4, out_specs=NEAR, out_sh...  3.58 us
    pallas_call x1, Pallas kernels, bypass(): pl.pallas_call(bypass_kernel, in_specs=[FAR, pl.BlockSpec(memory_space=pl...  2.98 us
    pallas_call x1, Pallas kernels, backward(): pl.pallas_call(backward_kernel, in_specs=[NEAR, NEAR, FAR, FAR], out_spec...  2.83 us
    all_to_all x1, waiting for transfers between devices, shards(): lax.all_to_all(mode_grads.reshape(SLABS, 1, 128), 'slab', 0, 0, tiled=True)  2.27 us
    pallas_call x1, Pallas kernels, middle(): pl.pallas_call(middle_kernel, in_specs=[NEAR] * 4, out_specs=(NEAR, NEAR)...  1.31 us
  transfers between devices with their start and end apart: 1, of which 1 were waited for; matrix products, arithmetic and copies ran while one was open for 1% of the time, Pallas kernels for 5%

profile of v2, /device:TPU:4, one launch (start us, length us, event | category | flops | bytes accessed | tf_op | source)
XLA Modules:
  0.0 59.0 jit_solution(221168424574349472)
XLA Ops:
  0.6 0.0 copy-start.1
  0.6 0.0 copy-start.2
  0.7 0.0 copy-start.3
  0.7 0.0 copy-start
  0.7 3.6 %to_plane_modes.1 = f32[256,128]{1,0:T(8,128)S(1)} custom-call(bf16[6,2,256,256]{3,2,1,0:T(8,128)(2,1)} %bitcast.25, bf16[6,2,256,256]{3,2,1,0:T(8,128)(2,1)} %bitcast.20, bf16[2,256,128]{2,1,0:T(8,128)(2,1)} %constant.14.clone.far_y_ref, bf16[128,256]{1,0:T(8,128)(2,1)} %constant.15.clone.far_x_ref), custom_call_target="tpu_custom_call" | custom-call | flops 1000000000 | bytes 3145728 | tf_op jit(solution)/shard_map/to_plane_modes/pallas_call | solution.py:285
  4.3 31.6 %all_to_all.10 = f32[128,2,128]{2,1,0:T(2,128)S(1)} all-to-all(f32[128,2,128]{2,1,0:T(2,128)S(1)} %bitcast.17), channel_id=1, replica_groups=mesh['slab'=128,'rep'=4] {'slab'}, dimensions={0} | all-to-all | bytes 262144 | tf_op jit(solution)/shard_map/all_to_all | solution.py:363
  35.9 0.0 copy-done.1
  35.9 0.0 copy-done.2
  35.9 0.0 copy-done.3
  35.9 1.3 %mode_products.1 = (f32[8,8,32]{2,1,0:T(8,128)S(1)}, f32[128,128]{1,0:T(8,128)}) custom-call(f32[256,128]{1,0:T(8,128)S(1)} %bitcast.16, f32[8,8,32]{2,1,0:T(8,128)S(1)} %bitcast.19, bf16[256,128]{1,0:T(8,128)(2,1)S(1)} %copy-done.3, bf16[128,384]{1,0:T(8,128)(2,1)S(1)} %copy-done.2), custom_call_target="tpu_custom_call" | custom-call | flops 100000000 | bytes 1048576 | tf_op jit(solution)/shard_map/mode_products/pallas_call | solution.py:305
  37.2 6.1 %all-to-all-start.1 = ((f32[128,1,128]{2,1,0:T(1,128)}), f32[128,1,128]{2,1,0:T(1,128)S(1)}, u32[]{:S(2)}, u32[]{:S(2)}) async-start(f32[128,1,128]{2,1,0:T(1,128)} %bitcast.6), calls=%async_computation.1 | async-start | bytes 131072 | tf_op jit(solution)/shard_map/all_to_all | solution.py:367
  43.4 7.0 %all-gather = f32[32,8,32]{2,1,0:T(8,128)S(1)} all-gather(f32[8,8,32]{2,1,0:T(8,128)S(1)} %get-tuple-element.9), channel_id=2, replica_groups=mesh['slab'=128,'rep'=4] {'rep'}, dimensions={0}, use_global_device_ids=true | all-gather | bytes 40960 | tf_op jit(solution)/shard_map/all_gather | solution.py:370
  50.3 0.6 %reduce_sum.9 = f32[8,8,32]{2,1,0:T(8,128)} reduce(f32[4,8,8,32]{3,2,1,0:T(8,128)S(1)} %bitcast.23, f32[]{:T(128)} %constant.6.clone.1), dimensions={0}, to_apply=%region_0.0 | reduce | flops 6144 | bytes 40964 | tf_op jit(solution)/shard_map/reduce_sum | solution.py:370
  51.0 0.0 copy-done
  51.0 3.0 %bypass.1.bypass_ref = f32[6,2,256,256]{3,2,1,0:T(8,128)S(1)} custom-call(bf16[6,2,256,256]{3,2,1,0:T(8,128)(2,1)} %bitcast.21, f32[8]{0:T(128)S(1)} %bitcast.18), custom_call_target="tpu_custom_call" | custom-call | flops 100000000 | bytes 6291456 | tf_op jit(solution)/shard_map/bypass/pallas_call | solution.py:321
  53.9 2.3 %all-to-all-done.1 = f32[128,1,128]{2,1,0:T(1,128)S(1)} async-done(((f32[128,1,128]{2,1,0:T(1,128)}), f32[128,1,128]{2,1,0:T(1,128)S(1)}, u32[]{:S(2)}, u32[]{:S(2)}) %all-to-all-start.1) | async-done | bytes 65568 | tf_op jit(solution)/shard_map/all_to_all | solution.py:367
  56.2 2.8 %to_input_grad.1 = bf16[6,2,256,256]{3,2,1,0:T(8,128)(2,1)} custom-call(f32[128,128]{1,0:T(8,128)S(1)} %bitcast.15, f32[6,2,256,256]{3,2,1,0:T(8,128)S(1)} %bypass.1.bypass_ref, bf16[256,512]{1,0:T(8,128)(2,1)} %constant.18.clone.far_y_ref, bf16[512,192]{1,0:T(8,128)(2,1)} %constant.19.clone.far_x_ref), custom_call_target="tpu_custom_call" | custom-call | flops 1000000000 | bytes 6291456 | tf_op jit(solution)/shard_map/to_input_grad/pallas_call | solution.py:338
Async XLA Ops:
  0.6 35.3 %copy-start.1 = (f32[8,8,1,1,32]{4,3,2,1,0:T(1,128)S(1)}, f32[8,8,1,1,32]{4,3,2,1,0:T(1,128)}, u32[]{:S(2)}) copy-start(f32[8,8,1,1,32]{4,3,2,1,0:T(1,128)} %param.12) | copy-start | bytes 24580
  0.6 35.3 %copy-start.2 = (bf16[128,384]{1,0:T(8,128)(2,1)S(1)}, bf16[128,384]{1,0:T(8,128)(2,1)}, u32[]{:S(2)}) copy-start(bf16[128,384]{1,0:T(8,128)(2,1)} %constant.17.clone.back_ref) | copy-start | bytes 294916
  0.7 35.2 %copy-start.3 = (bf16[256,128]{1,0:T(8,128)(2,1)S(1)}, bf16[256,128]{1,0:T(8,128)(2,1)}, u32[]{:S(2)}) copy-start(bf16[256,128]{1,0:T(8,128)(2,1)} %constant.16.clone.depth_ref) | copy-start | bytes 196612
  0.7 50.3 %copy-start = (f32[8,1,1]{0,2,1:T(1,128)S(1)}, f32[8,1,1]{0,2,1:T(1,128)}, u32[]{:S(2)}) copy-start(f32[8,1,1]{0,2,1:T(1,128)} %param.13) | copy-start | bytes 100
  37.2 19.0 %all-to-all-start.1 = ((f32[128,1,128]{2,1,0:T(1,128)}), f32[128,1,128]{2,1,0:T(1,128)S(1)}, u32[]{:S(2)}, u32[]{:S(2)}) async-start(f32[128,1,128]{2,1,0:T(1,128)} %bitcast.6), calls=%async_computation.1 | async-start | bytes 131072 | tf_op jit(solution)/shard_map/all_to_all | solution.py:367

commit v3 on v2

--- a/solution.py
+++ b/solution.py
@@ -52,11 +52,13 @@
     depth = np.concatenate(split(depth), axis=1)
     to_real = interleave(cos, -sin).T
     to_imag = interleave(sin, cos).T
-    high, low = split(np.concatenate([to_real, to_imag], axis=1))
-    inverse_y = np.concatenate([high, high, low, np.zeros_like(low)], axis=0)
-    high, low = split(np.block([[cos, -sin], [sin, cos]]))
-    inverse_x = np.concatenate([high, high, low], axis=1)
-    return forward_y, forward_x, depth, depth_back, inverse_y, inverse_x
+    inverse = np.zeros((N, 2 * N), ml_dtypes.bfloat16)
+    inverse[:128] = np.concatenate(split(np.concatenate([to_real, to_imag], axis=1)), axis=0)
+    inverse_x = np.concatenate(split(np.block([[cos, -sin], [sin, cos]])), axis=1)
+    for block in range(4):
+        place = slice(128 * block, 128 * block + 128)
+        inverse[128:, place] = inverse_x[place]
+    return forward_y, forward_x, depth, depth_back, inverse
 
 
 def dot(left, right):
@@ -194,13 +196,16 @@
     )
 
 
-def bypass_kernel(grad_ref, bypass_ref, out_ref, field, sems):
+def bypass_kernel(
+    grad_ref, bypass_ref, parts_ref, out_ref, sum_ref, field, sems
+):
     copies = [
         pltpu.make_async_copy(grad_ref.at[:, plane], field.at[:, plane], sems.at[plane])
         for plane in range(PLANES)
     ]
     for copy in copies:
         copy.start()
+    sum_ref[...] = (parts_ref[0] + parts_ref[1]) + (parts_ref[2] + parts_ref[3])
     weight = [bypass_ref[blade] for blade in range(8)]
     step = 32
     for plane in range(PLANES):
@@ -219,13 +224,13 @@
 
         lax.fori_loop(0, N // step, chunk, 0)
 
-def backward_kernel(
-    modes_ref, bypass_ref, far_y_ref, far_x_ref, out_ref, table_y, table_x, total_ref, near_sems, sems
-):
-    fetch_y = pltpu.make_async_copy(far_y_ref, table_y, near_sems.at[0])
-    fetch_x = pltpu.make_async_copy(far_x_ref, table_x, near_sems.at[1])
-    fetch_y.start()
-    fetch_x.start()
+def backward_kernel(modes_ref, bypass_ref, table_ref, out_ref, total_ref, sems):
+    high, low = table_ref[:64, :], table_ref[64:128, :]
+    table_y = jnp.concatenate([high, high, low, low], axis=0)
+    table_x = jnp.concatenate(
+        [table_ref[128:, 128 * block : 128 * block + 128] for block in range(4)], axis=0
+    )
+    table_x = jnp.concatenate([table_x, table_x], axis=1)
     low_half = lanes(KM) < 64
     slot = lanes(KM) // 16
     groups = [modes_ref[pl.ds(group, KM, stride=GROUPS), :] for group in range(GROUPS)]
@@ -237,24 +242,20 @@
                 value = roll(groups[place % GROUPS], 16 * (place - axis) - 64 * plane)
                 gathered = jnp.where(slot == place, value, gathered)
             high = gathered.astype(jnp.bfloat16).astype(jnp.float32)
-            first = jnp.where(low_half, high, gathered - high)
-            second = jnp.where(low_half, high, 0.0)
-            left.append(jnp.concatenate([first, second], axis=1).astype(jnp.bfloat16))
-    left = jnp.concatenate(left, axis=0)
-    fetch_y.wait()
-    fetch_x.wait()
-    along_y = dot(left, table_y[...])
+            both = jnp.where(low_half, high, gathered - high).astype(jnp.bfloat16)
+            left.append(jnp.concatenate([both, both], axis=1))
+    along_y = dot(jnp.concatenate(left, axis=0), table_y)
     right = []
     for part in range(3 * PLANES):
         rows = along_y[part * KM : (part + 1) * KM]
         rows = jnp.concatenate([rows[:, :N], rows[:, N:]], axis=0)
         high = rows.astype(jnp.bfloat16)
         low = (rows - high.astype(jnp.float32)).astype(jnp.bfloat16)
-        right.append(jnp.concatenate([high, low, high], axis=0))
+        right.append(jnp.concatenate([high, high, low, low], axis=0))
     copies = []
     for part in range(3 * PLANES):
         plane, axis = divmod(part, 3)
-        spectral = dot(table_x[...], right[part])
+        spectral = dot(table_x, right[part])
         for entry, rows in ((axis, spectral[:N]), (3 + axis, spectral[N:])):
             total = rows + bypass_ref[entry, plane]
             total_ref[entry, plane] = total.astype(jnp.bfloat16)
@@ -317,12 +318,15 @@
     )(planes, weight, depth, back)
 
 
-def bypass(grad, weight, interpret=False):
+def bypass(grad, weight, parts, interpret=False):
     return pl.pallas_call(
         bypass_kernel,
-        in_specs=[FAR, pl.BlockSpec(memory_space=pltpu.SMEM)],
-        out_specs=NEAR,
-        out_shape=jax.ShapeDtypeStruct((6, PLANES, N, N), jnp.float32),
+        in_specs=[FAR, pl.BlockSpec(memory_space=pltpu.SMEM), NEAR],
+        out_specs=(NEAR, NEAR),
+        out_shape=(
+            jax.ShapeDtypeStruct((6, PLANES, N, N), jnp.float32),
+            jax.ShapeDtypeStruct(parts.shape[1:], parts.dtype),
+        ),
         scratch_shapes=[
             pltpu.VMEM((6, PLANES, N, N), jnp.bfloat16),
             pltpu.SemaphoreType.DMA((PLANES,)),
@@ -331,31 +335,28 @@
         cost_estimate=cost(10**8, 6 * 2**20),
         interpret=interpret,
         name="bypass",
-    )(grad, weight)
-
-
-def backward(modes, bypassed, table_y, table_x, interpret=False):
+    )(grad, weight, parts)
+
+
+def backward(modes, bypassed, table, interpret=False):
     return pl.pallas_call(
         backward_kernel,
-        in_specs=[NEAR, NEAR, FAR, FAR],
+        in_specs=[NEAR] * 3,
         out_specs=FAR,
         out_shape=jax.ShapeDtypeStruct((6, PLANES, N, N), jnp.bfloat16),
         scratch_shapes=[
-            pltpu.VMEM((N, 2 * N), jnp.bfloat16),
-            pltpu.VMEM((2 * N, 192), jnp.bfloat16),
             pltpu.VMEM((6, PLANES, N, N), jnp.bfloat16),
-            pltpu.SemaphoreType.DMA((2,)),
             pltpu.SemaphoreType.DMA((6, PLANES)),
         ],
-        compiler_params=params(24),
-        cost_estimate=cost(10**9, 6 * 2**20),
+        compiler_params=params(16),
+        cost_estimate=cost(10**8, 2**20),
         interpret=interpret,
         name="to_input_grad",
-    )(modes, bypassed, table_y, table_x)
+    )(modes, bypassed, table)
 
 
 def shards(saved_input, output_grad, spectral_weight, bypass_weight):
-    forward_y, forward_x, depth, depth_back, inverse_y, inverse_x = tables()
+    forward_y, forward_x, depth, depth_back, inverse = tables()
     saved = saved_input.reshape(6, PLANES, N, N)
     grad = output_grad.reshape(6, PLANES, N, N)
     far = functools.partial(pltpu.with_memory_space_constraint, memory_space=pltpu.HBM)
@@ -365,10 +366,10 @@
         rows.reshape(SLABS * PLANES, 128), spectral_weight.reshape(8, 8, KM), depth, depth_back
     )
     back = lax.all_to_all(mode_grads.reshape(SLABS, 1, 128), "slab", 0, 0, tiled=True)
-    local_grad, later = lax.optimization_barrier((local_grad, grad))
-    bypassed = bypass(far(later), bypass_weight.reshape(8))
-    weight_grad = jnp.sum(lax.all_gather(local_grad, "rep"), axis=0)
-    input_grad = backward(back.reshape(SLABS, 128), bypassed, far(inverse_y), far(inverse_x))
+    bypassed, weight_grad = bypass(
+        far(grad), bypass_weight.reshape(8), lax.all_gather(local_grad, "rep")
+    )
+    input_grad = backward(back.reshape(SLABS, 128), bypassed, inverse)
     return (
         input_grad.reshape(1, 6, 1, PLANES, N, N),
         weight_grad.reshape(8, 8, 1, 1, KM),

time: 59.3 us -> 58.3 us (0.983)
  other arithmetic: 0.63 us -> 0 us
    pallas_call x1, Pallas kernels: 2.83 us -> 1.75 us  [backward(): pl.pallas_call(backward_kernel, in_specs=[NEAR] * 3, out_specs=FAR, out_s...]
    reduce_sum x1 -> x0, other arithmetic: 0.63 us -> none  [shards(): weight_grad = jnp.sum(lax.all_gather(local_grad, 'rep'), axis=0)]
  transfers between devices with their start and end apart: 1 -> 1, of which waited for: 1 -> 1; matrix products, arithmetic and copies ran while one was open for 1% -> 0% of each run, Pallas kernels for 5% -> 6%
where the time goes in v3:
time: 58.3 us; the launch traced here: 58.1 us
  blocking collectives  38.7 us (66%)
  Pallas kernels  10.2 us (17%)
  starting transfers between devices  6.15 us (11%)
  waiting for transfers between devices  2.36 us (4%)
  between operations  0.7 us (1%)
    all_to_all x1, blocking collectives, shards(): lax.all_to_all(modes.reshape(SLABS, PLANES, 128), 'slab', 0, 0, tiled=True)  31.8 us
    all_gather x1, blocking collectives, shards(): lax.all_gather(local_grad, 'rep')  6.96 us
    all_to_all x1, starting transfers between devices, shards(): lax.all_to_all(mode_grads.reshape(SLABS, 1, 128), 'slab', 0, 0, tiled=True)  6.15 us
    pallas_call x1, Pallas kernels, forward(): pl.pallas_call(forward_kernel, in_specs=[FAR] * 4, out_specs=NEAR, out_sh...  3.58 us
    pallas_call x1, Pallas kernels, bypass(): pl.pallas_call(bypass_kernel, in_specs=[FAR, pl.BlockSpec(memory_space=pl...  3.52 us
    all_to_all x1, waiting for transfers between devices, shards(): lax.all_to_all(mode_grads.reshape(SLABS, 1, 128), 'slab', 0, 0, tiled=True)  2.36 us
    pallas_call x1, Pallas kernels, backward(): pl.pallas_call(backward_kernel, in_specs=[NEAR] * 3, out_specs=FAR, out_s...  1.75 us
    pallas_call x1, Pallas kernels, middle(): pl.pallas_call(middle_kernel, in_specs=[NEAR] * 4, out_specs=(NEAR, NEAR)...  1.31 us
  transfers between devices with their start and end apart: 1, of which 1 were waited for; matrix products, arithmetic and copies ran while one was open for 0% of the time, Pallas kernels for 6%

profile of v3, /device:TPU:4, one launch (start us, length us, event | category | flops | bytes accessed | tf_op | source)
XLA Modules:
  0.0 58.1 jit_solution(9856319390050851305)
XLA Ops:
  0.6 0.0 copy-start.2
  0.6 0.0 copy-start.3
  0.7 0.0 copy-start.4
  0.7 0.0 copy-start.1
  0.7 3.6 %to_plane_modes.1 = f32[256,128]{1,0:T(8,128)S(1)} custom-call(bf16[6,2,256,256]{3,2,1,0:T(8,128)(2,1)} %bitcast.26, bf16[6,2,256,256]{3,2,1,0:T(8,128)(2,1)} %bitcast.24, bf16[2,256,128]{2,1,0:T(8,128)(2,1)} %constant.10.clone.far_y_ref, bf16[128,256]{1,0:T(8,128)(2,1)} %constant.11.clone.far_x_ref), custom_call_target="tpu_custom_call" | custom-call | flops 1000000000 | bytes 3145728 | tf_op jit(solution)/shard_map/to_plane_modes/pallas_call | solution.py:286
  4.3 0.0 copy-start
  4.3 31.8 %all_to_all.10 = f32[128,2,128]{2,1,0:T(2,128)S(1)} all-to-all(f32[128,2,128]{2,1,0:T(2,128)S(1)} %bitcast.20), channel_id=1, replica_groups=mesh['slab'=128,'rep'=4] {'slab'}, dimensions={0} | all-to-all | bytes 262144 | tf_op jit(solution)/shard_map/all_to_all | solution.py:364
  36.0 0.0 copy-done.2
  36.0 0.0 copy-done.3
  36.0 0.0 copy-done.4
  36.0 1.3 %mode_products.1 = (f32[8,8,32]{2,1,0:T(8,128)S(1)}, f32[128,128]{1,0:T(8,128)}) custom-call(f32[256,128]{1,0:T(8,128)S(1)} %bitcast.19, f32[8,8,32]{2,1,0:T(8,128)S(1)} %bitcast.22, bf16[256,128]{1,0:T(8,128)(2,1)S(1)} %copy-done.4, bf16[128,384]{1,0:T(8,128)(2,1)S(1)} %copy-done.3), custom_call_target="tpu_custom_call" | custom-call | flops 100000000 | bytes 1048576 | tf_op jit(solution)/shard_map/mode_products/pallas_call | solution.py:306
  37.4 6.1 %all-to-all-start.1 = ((f32[128,1,128]{2,1,0:T(1,128)}), f32[128,1,128]{2,1,0:T(1,128)S(1)}, u32[]{:S(2)}, u32[]{:S(2)}) async-start(f32[128,1,128]{2,1,0:T(1,128)} %bitcast.6), calls=%async_computation.1 | async-start | bytes 131072 | tf_op jit(solution)/shard_map/all_to_all | solution.py:368
  43.5 7.0 %all-gather = f32[32,8,32]{2,1,0:T(8,128)S(1)} all-gather(f32[8,8,32]{2,1,0:T(8,128)S(1)} %get-tuple-element.7), channel_id=2, replica_groups=mesh['slab'=128,'rep'=4] {'rep'}, dimensions={0}, use_global_device_ids=true | all-gather | bytes 40960 | tf_op jit(solution)/shard_map/all_gather | solution.py:370
  50.5 0.0 copy-done.1
  50.5 3.5 %bypass.1 = (f32[6,2,256,256]{3,2,1,0:T(8,128)S(1)}, f32[8,8,32]{2,1,0:T(8,128)}) custom-call(bf16[6,2,256,256]{3,2,1,0:T(8,128)(2,1)} %bitcast.25, f32[8]{0:T(128)S(1)} %bitcast.21, f32[4,8,8,32]{3,2,1,0:T(8,128)S(1)} %bitcast.17), custom_call_target="tpu_custom_call" | custom-call | flops 100000000 | bytes 6291456 | tf_op jit(solution)/shard_map/bypass/pallas_call | solution.py:322
  54.0 2.4 %all-to-all-done.1 = f32[128,1,128]{2,1,0:T(1,128)S(1)} async-done(((f32[128,1,128]{2,1,0:T(1,128)}), f32[128,1,128]{2,1,0:T(1,128)S(1)}, u32[]{:S(2)}, u32[]{:S(2)}) %all-to-all-start.1) | async-done | bytes 65568 | tf_op jit(solution)/shard_map/all_to_all | solution.py:368
  56.4 0.0 copy-done
  56.4 1.7 %to_input_grad.1 = bf16[6,2,256,256]{3,2,1,0:T(8,128)(2,1)} custom-call(f32[128,128]{1,0:T(8,128)S(1)} %bitcast.18, f32[6,2,256,256]{3,2,1,0:T(8,128)S(1)} %get-tuple-element.8.bypass_ref, bf16[256,512]{1,0:T(8,128)(2,1)S(1)} %copy-done), custom_call_target="tpu_custom_call" | custom-call | flops 100000000 | bytes 1048576 | tf_op jit(solution)/shard_map/to_input_grad/pallas_call | solution.py:342
Async XLA Ops:
  0.6 35.4 %copy-start.2 = (f32[8,8,1,1,32]{4,3,2,1,0:T(1,128)S(1)}, f32[8,8,1,1,32]{4,3,2,1,0:T(1,128)}, u32[]{:S(2)}) copy-start(f32[8,8,1,1,32]{4,3,2,1,0:T(1,128)} %param.11) | copy-start | bytes 24580
  0.6 35.4 %copy-start.3 = (bf16[128,384]{1,0:T(8,128)(2,1)S(1)}, bf16[128,384]{1,0:T(8,128)(2,1)}, u32[]{:S(2)}) copy-start(bf16[128,384]{1,0:T(8,128)(2,1)} %constant.13.clone.back_ref) | copy-start | bytes 294916
  0.7 35.4 %copy-start.4 = (bf16[256,128]{1,0:T(8,128)(2,1)S(1)}, bf16[256,128]{1,0:T(8,128)(2,1)}, u32[]{:S(2)}) copy-start(bf16[256,128]{1,0:T(8,128)(2,1)} %constant.12.clone.depth_ref) | copy-start | bytes 196612
  0.7 49.8 %copy-start.1 = (f32[8,1,1]{0,2,1:T(1,128)S(1)}, f32[8,1,1]{0,2,1:T(1,128)}, u32[]{:S(2)}) copy-start(f32[8,1,1]{0,2,1:T(1,128)} %param.12) | copy-start | bytes 100
  4.3 52.1 %copy-start = (bf16[256,512]{1,0:T(8,128)(2,1)S(1)}, bf16[256,512]{1,0:T(8,128)(2,1)}, u32[]{:S(2)}) copy-start(bf16[256,512]{1,0:T(8,128)(2,1)} %constant.14.clone.table_ref) | copy-start | bytes 786436
  37.4 19.0 %all-to-all-start.1 = ((f32[128,1,128]{2,1,0:T(1,128)}), f32[128,1,128]{2,1,0:T(1,128)S(1)}, u32[]{:S(2)}, u32[]{:S(2)}) async-start(f32[128,1,128]{2,1,0:T(1,128)} %bitcast.6), calls=%async_computation.1 | async-start | bytes 131072 | tf_op jit(solution)/shard_map/all_to_all | solution.py:368

commit v4 on v3

--- a/solution.py
+++ b/solution.py
@@ -75,31 +75,29 @@
 
 
 def forward_kernel(saved_ref, grad_ref, far_y_ref, far_x_ref, out_ref, fields, table_y, table_x, rows_ref, sems):
-    copies = [
-        pltpu.make_async_copy(far_y_ref, table_y, sems.at[0]),
-        pltpu.make_async_copy(far_x_ref, table_x, sems.at[1]),
-    ]
-    for field, ref in enumerate((saved_ref, grad_ref)):
-        for entry in range(6):
-            copies.append(
-                pltpu.make_async_copy(
-                    ref.at[entry], fields.at[field, entry], sems.at[2 + 6 * field + entry]
-                )
-            )
-    for copy in copies:
-        copy.start()
-    for copy in copies:
-        copy.wait()
+    near_y = pltpu.make_async_copy(far_y_ref, table_y, sems.at[0])
+    near_x = pltpu.make_async_copy(far_x_ref, table_x, sems.at[1])
+    near_saved = pltpu.make_async_copy(saved_ref, fields.at[0], sems.at[2])
+    near_grad = pltpu.make_async_copy(grad_ref, fields.at[1], sems.at[3])
+    near_y.start()
+    near_x.start()
+    for entry in range(6):
+        pltpu.make_async_copy(saved_ref.at[entry], fields.at[0, entry], sems.at[2]).start()
+    near_grad.start()
+    near_y.wait()
+    near_x.wait()
     is_real = (lanes(KM) // 8) % 2 == 0
     slot = lanes(KM) // 16
-    places = [(field, axis) for field in range(2) for axis in range(3)]
-    for place, (field, axis) in enumerate(places):
-        real = fields[field, axis].reshape(PLANES * N, N)
-        imag = fields[field, 3 + axis].reshape(PLANES * N, N)
-        rows = dot(real, table_y[0]) + dot(imag, table_y[1])
-        high = rows.astype(jnp.bfloat16)
-        rows_ref[place, :, :128] = high
-        rows_ref[place, :, 128:] = (rows - high.astype(jnp.float32)).astype(jnp.bfloat16)
+    for field, whole_field in enumerate((near_saved, near_grad)):
+        whole_field.wait()
+        for axis in range(3):
+            place = 3 * field + axis
+            real = fields[field, axis].reshape(PLANES * N, N)
+            imag = fields[field, 3 + axis].reshape(PLANES * N, N)
+            rows = dot(real, table_y[0]) + dot(imag, table_y[1])
+            high = rows.astype(jnp.bfloat16)
+            rows_ref[place, :, :128] = high
+            rows_ref[place, :, 128:] = (rows - high.astype(jnp.float32)).astype(jnp.bfloat16)
     for plane in range(PLANES):
         modes = []
         for place in range(6):
@@ -224,7 +222,7 @@
 
         lax.fori_loop(0, N // step, chunk, 0)
 
-def backward_kernel(modes_ref, bypass_ref, table_ref, out_ref, total_ref, sems):
+def backward_kernel(modes_ref, bypass_ref, table_ref, out_ref, total_ref, sem):
     high, low = table_ref[:64, :], table_ref[64:128, :]
     table_y = jnp.concatenate([high, high, low, low], axis=0)
     table_x = jnp.concatenate(
@@ -252,7 +250,6 @@
         high = rows.astype(jnp.bfloat16)
         low = (rows - high.astype(jnp.float32)).astype(jnp.bfloat16)
         right.append(jnp.concatenate([high, high, low, low], axis=0))
-    copies = []
     for part in range(3 * PLANES):
         plane, axis = divmod(part, 3)
         spectral = dot(table_x, right[part])
@@ -260,14 +257,10 @@
             total = rows + bypass_ref[entry, plane]
             total_ref[entry, plane] = total.astype(jnp.bfloat16)
         for entry in (axis, 3 + axis):
-            copies.append(
-                pltpu.make_async_copy(
-                    total_ref.at[entry, plane], out_ref.at[entry, plane], sems.at[entry, plane]
-                )
-            )
-            copies[-1].start()
-    for copy in copies:
-        copy.wait()
+            pltpu.make_async_copy(
+                total_ref.at[entry, plane], out_ref.at[entry, plane], sem
+            ).start()
+    pltpu.make_async_copy(total_ref, out_ref, sem).wait()
 
 
 NEAR = pl.BlockSpec(memory_space=pltpu.VMEM)
@@ -293,7 +286,7 @@
             pltpu.VMEM((2, N, 128), jnp.bfloat16),
             pltpu.VMEM((128, N), jnp.bfloat16),
             pltpu.VMEM((6, PLANES * N, N), jnp.bfloat16),
-            pltpu.SemaphoreType.DMA((14,)),
+            pltpu.SemaphoreType.DMA((4,)),
         ],
         compiler_params=params(24),
         cost_estimate=cost(10**9, 3 * 2**20),
@@ -346,7 +339,7 @@
         out_shape=jax.ShapeDtypeStruct((6, PLANES, N, N), jnp.bfloat16),
         scratch_shapes=[
             pltpu.VMEM((6, PLANES, N, N), jnp.bfloat16),
-            pltpu.SemaphoreType.DMA((6, PLANES)),
+            pltpu.SemaphoreType.DMA(()),
         ],
         compiler_params=params(16),
         cost_estimate=cost(10**8, 2**20),

time: 58.3 us -> 58 us (level)
  no operation moved by 1% of the time
where the time goes in v4:
time: 58 us; the launch traced here: 57.8 us
  blocking collectives  38.7 us (67%)
  Pallas kernels  9.87 us (17%)
  starting transfers between devices  6.15 us (11%)
  waiting for transfers between devices  2.36 us (4%)
  between operations  0.7 us (1%)
    all_to_all x1, blocking collectives, shards(): lax.all_to_all(modes.reshape(SLABS, PLANES, 128), 'slab', 0, 0, tiled=True)  31.8 us
    all_gather x1, blocking collectives, shards(): lax.all_gather(local_grad, 'rep')  6.96 us
    all_to_all x1, starting transfers between devices, shards(): lax.all_to_all(mode_grads.reshape(SLABS, 1, 128), 'slab', 0, 0, tiled=True)  6.15 us
    pallas_call x1, Pallas kernels, bypass(): pl.pallas_call(bypass_kernel, in_specs=[FAR, pl.BlockSpec(memory_space=pl...  3.52 us
    pallas_call x1, Pallas kernels, forward(): pl.pallas_call(forward_kernel, in_specs=[FAR] * 4, out_specs=NEAR, out_sh...  3.4 us
    all_to_all x1, waiting for transfers between devices, shards(): lax.all_to_all(mode_grads.reshape(SLABS, 1, 128), 'slab', 0, 0, tiled=True)  2.36 us
    pallas_call x1, Pallas kernels, backward(): pl.pallas_call(backward_kernel, in_specs=[NEAR] * 3, out_specs=FAR, out_s...  1.64 us
    pallas_call x1, Pallas kernels, middle(): pl.pallas_call(middle_kernel, in_specs=[NEAR] * 4, out_specs=(NEAR, NEAR)...  1.31 us
  transfers between devices with their start and end apart: 1, of which 1 were waited for; matrix products, arithmetic and copies ran while one was open for 0% of the time, Pallas kernels for 6%

profile of v4, /device:TPU:4, one launch (start us, length us, event | category | flops | bytes accessed | tf_op | source)
XLA Modules:
  0.0 57.8 jit_solution(4062257582792558201)
XLA Ops:
  0.6 0.0 copy-start.2
  0.6 0.0 copy-start.3
  0.7 0.0 copy-start.4
  0.7 0.0 copy-start.1
  0.7 3.4 %to_plane_modes.1 = f32[256,128]{1,0:T(8,128)S(1)} custom-call(bf16[6,2,256,256]{3,2,1,0:T(8,128)(2,1)} %bitcast.26, bf16[6,2,256,256]{3,2,1,0:T(8,128)(2,1)} %bitcast.24, bf16[2,256,128]{2,1,0:T(8,128)(2,1)} %constant.10.clone.far_y_ref, bf16[128,256]{1,0:T(8,128)(2,1)} %constant.11.clone.far_x_ref), custom_call_target="tpu_custom_call" | custom-call | flops 1000000000 | bytes 3145728 | tf_op jit(solution)/shard_map/to_plane_modes/pallas_call | solution.py:279
  4.1 0.0 copy-start
  4.1 31.8 %all_to_all.10 = f32[128,2,128]{2,1,0:T(2,128)S(1)} all-to-all(f32[128,2,128]{2,1,0:T(2,128)S(1)} %bitcast.20), channel_id=1, replica_groups=mesh['slab'=128,'rep'=4] {'slab'}, dimensions={0} | all-to-all | bytes 262144 | tf_op jit(solution)/shard_map/all_to_all | solution.py:357
  35.8 0.0 copy-done.2
  35.8 0.0 copy-done.3
  35.8 0.0 copy-done.4
  35.9 1.3 %mode_products.1 = (f32[8,8,32]{2,1,0:T(8,128)S(1)}, f32[128,128]{1,0:T(8,128)}) custom-call(f32[256,128]{1,0:T(8,128)S(1)} %bitcast.19, f32[8,8,32]{2,1,0:T(8,128)S(1)} %bitcast.22, bf16[256,128]{1,0:T(8,128)(2,1)S(1)} %copy-done.4, bf16[128,384]{1,0:T(8,128)(2,1)S(1)} %copy-done.3), custom_call_target="tpu_custom_call" | custom-call | flops 100000000 | bytes 1048576 | tf_op jit(solution)/shard_map/mode_products/pallas_call | solution.py:299
  37.2 6.1 %all-to-all-start.1 = ((f32[128,1,128]{2,1,0:T(1,128)}), f32[128,1,128]{2,1,0:T(1,128)S(1)}, u32[]{:S(2)}, u32[]{:S(2)}) async-start(f32[128,1,128]{2,1,0:T(1,128)} %bitcast.6), calls=%async_computation.1 | async-start | bytes 131072 | tf_op jit(solution)/shard_map/all_to_all | solution.py:361
  43.3 7.0 %all-gather = f32[32,8,32]{2,1,0:T(8,128)S(1)} all-gather(f32[8,8,32]{2,1,0:T(8,128)S(1)} %get-tuple-element.7), channel_id=2, replica_groups=mesh['slab'=128,'rep'=4] {'rep'}, dimensions={0}, use_global_device_ids=true | all-gather | bytes 40960 | tf_op jit(solution)/shard_map/all_gather | solution.py:363
  50.3 0.0 copy-done.1
  50.3 3.5 %bypass.1 = (f32[6,2,256,256]{3,2,1,0:T(8,128)S(1)}, f32[8,8,32]{2,1,0:T(8,128)}) custom-call(bf16[6,2,256,256]{3,2,1,0:T(8,128)(2,1)} %bitcast.25, f32[8]{0:T(128)S(1)} %bitcast.21, f32[4,8,8,32]{3,2,1,0:T(8,128)S(1)} %bitcast.17), custom_call_target="tpu_custom_call" | custom-call | flops 100000000 | bytes 6291456 | tf_op jit(solution)/shard_map/bypass/pallas_call | solution.py:315
  53.8 2.4 %all-to-all-done.1 = f32[128,1,128]{2,1,0:T(1,128)S(1)} async-done(((f32[128,1,128]{2,1,0:T(1,128)}), f32[128,1,128]{2,1,0:T(1,128)S(1)}, u32[]{:S(2)}, u32[]{:S(2)}) %all-to-all-start.1) | async-done | bytes 65568 | tf_op jit(solution)/shard_map/all_to_all | solution.py:361
  56.2 0.0 copy-done
  56.2 1.6 %to_input_grad.1 = bf16[6,2,256,256]{3,2,1,0:T(8,128)(2,1)} custom-call(f32[128,128]{1,0:T(8,128)S(1)} %bitcast.18, f32[6,2,256,256]{3,2,1,0:T(8,128)S(1)} %get-tuple-element.8.bypass_ref, bf16[256,512]{1,0:T(8,128)(2,1)S(1)} %copy-done), custom_call_target="tpu_custom_call" | custom-call | flops 100000000 | bytes 1048576 | tf_op jit(solution)/shard_map/to_input_grad/pallas_call | solution.py:335
Async XLA Ops:
  0.6 35.2 %copy-start.2 = (f32[8,8,1,1,32]{4,3,2,1,0:T(1,128)S(1)}, f32[8,8,1,1,32]{4,3,2,1,0:T(1,128)}, u32[]{:S(2)}) copy-start(f32[8,8,1,1,32]{4,3,2,1,0:T(1,128)} %param.11) | copy-start | bytes 24580
  0.6 35.2 %copy-start.3 = (bf16[128,384]{1,0:T(8,128)(2,1)S(1)}, bf16[128,384]{1,0:T(8,128)(2,1)}, u32[]{:S(2)}) copy-start(bf16[128,384]{1,0:T(8,128)(2,1)} %constant.13.clone.back_ref) | copy-start | bytes 294916
  0.7 35.2 %copy-start.4 = (bf16[256,128]{1,0:T(8,128)(2,1)S(1)}, bf16[256,128]{1,0:T(8,128)(2,1)}, u32[]{:S(2)}) copy-start(bf16[256,128]{1,0:T(8,128)(2,1)} %constant.12.clone.depth_ref) | copy-start | bytes 196612
  0.7 49.6 %copy-start.1 = (f32[8,1,1]{0,2,1:T(1,128)S(1)}, f32[8,1,1]{0,2,1:T(1,128)}, u32[]{:S(2)}) copy-start(f32[8,1,1]{0,2,1:T(1,128)} %param.12) | copy-start | bytes 100
  4.1 52.1 %copy-start = (bf16[256,512]{1,0:T(8,128)(2,1)S(1)}, bf16[256,512]{1,0:T(8,128)(2,1)}, u32[]{:S(2)}) copy-start(bf16[256,512]{1,0:T(8,128)(2,1)} %constant.14.clone.table_ref) | copy-start | bytes 786436
  37.2 19.0 %all-to-all-start.1 = ((f32[128,1,128]{2,1,0:T(1,128)}), f32[128,1,128]{2,1,0:T(1,128)S(1)}, u32[]{:S(2)}, u32[]{:S(2)}) async-start(f32[128,1,128]{2,1,0:T(1,128)} %bitcast.6), calls=%async_computation.1 | async-start | bytes 131072 | tf_op jit(solution)/shard_map/all_to_all | solution.py:361

commit v5 on v4

--- a/solution.py
+++ b/solution.py
@@ -44,8 +44,8 @@
     cos, sin = circle(np.arange(N))
     from_real = np.concatenate(split(interleave(cos, -sin)), axis=1)
     from_imag = np.concatenate(split(interleave(sin, cos)), axis=1)
-    forward_y = np.stack([from_real, from_imag])
     forward_x = np.concatenate(split(np.concatenate([cos.T, sin.T], axis=0)), axis=0)
+    forward_table = np.stack([from_real, from_imag, np.concatenate([forward_x[:, :128], forward_x[:, 128:]])])
     depth = np.concatenate([cos, sin], axis=1) * SCALE
     high, low = split(np.concatenate([depth[0::2], depth[1::2]], axis=1))
     depth_back = np.concatenate([high, high, low], axis=1)
@@ -58,7 +58,7 @@
     for block in range(4):
         place = slice(128 * block, 128 * block + 128)
         inverse[128:, place] = inverse_x[place]
-    return forward_y, forward_x, depth, depth_back, inverse
+    return forward_table, depth, depth_back, inverse
 
 
 def dot(left, right):
@@ -74,18 +74,16 @@
     return value if shift == 0 else pltpu.roll(value, shift, 1)
 
 
-def forward_kernel(saved_ref, grad_ref, far_y_ref, far_x_ref, out_ref, fields, table_y, table_x, rows_ref, sems):
-    near_y = pltpu.make_async_copy(far_y_ref, table_y, sems.at[0])
-    near_x = pltpu.make_async_copy(far_x_ref, table_x, sems.at[1])
-    near_saved = pltpu.make_async_copy(saved_ref, fields.at[0], sems.at[2])
-    near_grad = pltpu.make_async_copy(grad_ref, fields.at[1], sems.at[3])
-    near_y.start()
-    near_x.start()
+def forward_kernel(saved_ref, grad_ref, far_ref, out_ref, fields, table_ref, rows_ref, sems):
+    near_table = pltpu.make_async_copy(far_ref, table_ref, sems.at[0])
+    near_saved = pltpu.make_async_copy(saved_ref, fields.at[0], sems.at[1])
+    near_grad = pltpu.make_async_copy(grad_ref, fields.at[1], sems.at[2])
+    near_table.start()
     for entry in range(6):
-        pltpu.make_async_copy(saved_ref.at[entry], fields.at[0, entry], sems.at[2]).start()
+        pltpu.make_async_copy(saved_ref.at[entry], fields.at[0, entry], sems.at[1]).start()
     near_grad.start()
-    near_y.wait()
-    near_x.wait()
+    near_table.wait()
+    table_x = jnp.concatenate([table_ref[2, :128], table_ref[2, 128:]], axis=1)
     is_real = (lanes(KM) // 8) % 2 == 0
     slot = lanes(KM) // 16
     for field, whole_field in enumerate((near_saved, near_grad)):
@@ -94,14 +92,14 @@
             place = 3 * field + axis
             real = fields[field, axis].reshape(PLANES * N, N)
             imag = fields[field, 3 + axis].reshape(PLANES * N, N)
-            rows = dot(real, table_y[0]) + dot(imag, table_y[1])
+            rows = dot(real, table_ref[0]) + dot(imag, table_ref[1])
             high = rows.astype(jnp.bfloat16)
             rows_ref[place, :, :128] = high
             rows_ref[place, :, 128:] = (rows - high.astype(jnp.float32)).astype(jnp.bfloat16)
     for plane in range(PLANES):
         modes = []
         for place in range(6):
-            both = dot(table_x[...], rows_ref[place, plane * N : (plane + 1) * N, :])
+            both = dot(table_x, rows_ref[place, plane * N : (plane + 1) * N, :])
             both = both[:64] + both[64:]
             both = both[:, :128] + both[:, 128:]
             both = both + roll(both, 64)
@@ -275,24 +273,23 @@
     return pl.CostEstimate(flops=flops, bytes_accessed=moved, transcendentals=0)
 
 
-def forward(saved, grad, table_y, table_x, interpret=False):
+def forward(saved, grad, table, interpret=False):
     return pl.pallas_call(
         forward_kernel,
-        in_specs=[FAR] * 4,
+        in_specs=[FAR] * 3,
         out_specs=NEAR,
         out_shape=jax.ShapeDtypeStruct((SLABS * PLANES, 128), jnp.float32),
         scratch_shapes=[
             pltpu.VMEM((2, 6, PLANES, N, N), jnp.bfloat16),
-            pltpu.VMEM((2, N, 128), jnp.bfloat16),
-            pltpu.VMEM((128, N), jnp.bfloat16),
+            pltpu.VMEM((3, N, 128), jnp.bfloat16),
             pltpu.VMEM((6, PLANES * N, N), jnp.bfloat16),
-            pltpu.SemaphoreType.DMA((4,)),
+            pltpu.SemaphoreType.DMA((3,)),
         ],
         compiler_params=params(24),
         cost_estimate=cost(10**9, 3 * 2**20),
         interpret=interpret,
         name="to_plane_modes",
-    )(saved, grad, table_y, table_x)
+    )(saved, grad, table)
 
 
 def middle(planes, weight, depth, back, interpret=False):
@@ -349,11 +346,11 @@
 
 
 def shards(saved_input, output_grad, spectral_weight, bypass_weight):
-    forward_y, forward_x, depth, depth_back, inverse = tables()
+    forward_table, depth, depth_back, inverse = tables()
     saved = saved_input.reshape(6, PLANES, N, N)
     grad = output_grad.reshape(6, PLANES, N, N)
     far = functools.partial(pltpu.with_memory_space_constraint, memory_space=pltpu.HBM)
-    modes = forward(far(saved), far(grad), far(forward_y), far(forward_x))
+    modes = forward(far(saved), far(grad), far(forward_table))
     rows = lax.all_to_all(modes.reshape(SLABS, PLANES, 128), "slab", 0, 0, tiled=True)
     local_grad, mode_grads = middle(
         rows.reshape(SLABS * PLANES, 128), spectral_weight.reshape(8, 8, KM), depth, depth_back

time: 58 us -> 58 us (level)
  no operation moved by 1% of the time
where the time goes in v5:
time: 58 us; the launch traced here: 57.8 us
  blocking collectives  38.7 us (67%)
  Pallas kernels  9.86 us (17%)
  starting transfers between devices  6.15 us (11%)
  waiting for transfers between devices  2.36 us (4%)
  between operations  0.7 us (1%)
    all_to_all x1, blocking collectives, shards(): lax.all_to_all(modes.reshape(SLABS, PLANES, 128), 'slab', 0, 0, tiled=True)  31.8 us
    all_gather x1, blocking collectives, shards(): lax.all_gather(local_grad, 'rep')  6.96 us
    all_to_all x1, starting transfers between devices, shards(): lax.all_to_all(mode_grads.reshape(SLABS, 1, 128), 'slab', 0, 0, tiled=True)  6.15 us
    pallas_call x1, Pallas kernels, bypass(): pl.pallas_call(bypass_kernel, in_specs=[FAR, pl.BlockSpec(memory_space=pl...  3.52 us
    pallas_call x1, Pallas kernels, forward(): pl.pallas_call(forward_kernel, in_specs=[FAR] * 3, out_specs=NEAR, out_sh...  3.38 us
    all_to_all x1, waiting for transfers between devices, shards(): lax.all_to_all(mode_grads.reshape(SLABS, 1, 128), 'slab', 0, 0, tiled=True)  2.36 us
    pallas_call x1, Pallas kernels, backward(): pl.pallas_call(backward_kernel, in_specs=[NEAR] * 3, out_specs=FAR, out_s...  1.65 us
    pallas_call x1, Pallas kernels, middle(): pl.pallas_call(middle_kernel, in_specs=[NEAR] * 4, out_specs=(NEAR, NEAR)...  1.31 us
  transfers between devices with their start and end apart: 1, of which 1 were waited for; matrix products, arithmetic and copies ran while one was open for 0% of the time, Pallas kernels for 6%

profile of v5, /device:TPU:4, one launch (start us, length us, event | category | flops | bytes accessed | tf_op | source)
XLA Modules:
  0.0 57.8 jit_solution(1968462280449124948)
XLA Ops:
  0.6 0.0 copy-start.2
  0.6 0.0 copy-start.3
  0.7 0.0 copy-start.4
  0.7 0.0 copy-start.1
  0.7 3.4 %to_plane_modes.1 = f32[256,128]{1,0:T(8,128)S(1)} custom-call(bf16[6,2,256,256]{3,2,1,0:T(8,128)(2,1)} %bitcast.26, bf16[6,2,256,256]{3,2,1,0:T(8,128)(2,1)} %bitcast.24, bf16[3,256,128]{2,1,0:T(8,128)(2,1)} %constant.8.clone.far_ref), custom_call_target="tpu_custom_call" | custom-call | flops 1000000000 | bytes 3145728 | tf_op jit(solution)/shard_map/to_plane_modes/pallas_call | solution.py:277
  4.1 0.0 copy-start
  4.1 31.8 %all_to_all.10 = f32[128,2,128]{2,1,0:T(2,128)S(1)} all-to-all(f32[128,2,128]{2,1,0:T(2,128)S(1)} %bitcast.20), channel_id=1, replica_groups=mesh['slab'=128,'rep'=4] {'slab'}, dimensions={0} | all-to-all | bytes 262144 | tf_op jit(solution)/shard_map/all_to_all | solution.py:354
  35.8 0.0 copy-done.2
  35.8 0.0 copy-done.3
  35.8 0.0 copy-done.4
  35.8 1.3 %mode_products.1 = (f32[8,8,32]{2,1,0:T(8,128)S(1)}, f32[128,128]{1,0:T(8,128)}) custom-call(f32[256,128]{1,0:T(8,128)S(1)} %bitcast.19, f32[8,8,32]{2,1,0:T(8,128)S(1)} %bitcast.22, bf16[256,128]{1,0:T(8,128)(2,1)S(1)} %copy-done.4, bf16[128,384]{1,0:T(8,128)(2,1)S(1)} %copy-done.3), custom_call_target="tpu_custom_call" | custom-call | flops 100000000 | bytes 1048576 | tf_op jit(solution)/shard_map/mode_products/pallas_call | solution.py:296
  37.1 6.1 %all-to-all-start.1 = ((f32[128,1,128]{2,1,0:T(1,128)}), f32[128,1,128]{2,1,0:T(1,128)S(1)}, u32[]{:S(2)}, u32[]{:S(2)}) async-start(f32[128,1,128]{2,1,0:T(1,128)} %bitcast.6), calls=%async_computation.1 | async-start | bytes 131072 | tf_op jit(solution)/shard_map/all_to_all | solution.py:358
  43.3 7.0 %all-gather = f32[32,8,32]{2,1,0:T(8,128)S(1)} all-gather(f32[8,8,32]{2,1,0:T(8,128)S(1)} %get-tuple-element.7), channel_id=2, replica_groups=mesh['slab'=128,'rep'=4] {'rep'}, dimensions={0}, use_global_device_ids=true | all-gather | bytes 40960 | tf_op jit(solution)/shard_map/all_gather | solution.py:360
  50.3 0.0 copy-done.1
  50.3 3.5 %bypass.1 = (f32[6,2,256,256]{3,2,1,0:T(8,128)S(1)}, f32[8,8,32]{2,1,0:T(8,128)}) custom-call(bf16[6,2,256,256]{3,2,1,0:T(8,128)(2,1)} %bitcast.25, f32[8]{0:T(128)S(1)} %bitcast.21, f32[4,8,8,32]{3,2,1,0:T(8,128)S(1)} %bitcast.17), custom_call_target="tpu_custom_call" | custom-call | flops 100000000 | bytes 6291456 | tf_op jit(solution)/shard_map/bypass/pallas_call | solution.py:312
  53.8 2.4 %all-to-all-done.1 = f32[128,1,128]{2,1,0:T(1,128)S(1)} async-done(((f32[128,1,128]{2,1,0:T(1,128)}), f32[128,1,128]{2,1,0:T(1,128)S(1)}, u32[]{:S(2)}, u32[]{:S(2)}) %all-to-all-start.1) | async-done | bytes 65568 | tf_op jit(solution)/shard_map/all_to_all | solution.py:358
  56.2 0.0 copy-done
  56.2 1.6 %to_input_grad.1 = bf16[6,2,256,256]{3,2,1,0:T(8,128)(2,1)} custom-call(f32[128,128]{1,0:T(8,128)S(1)} %bitcast.18, f32[6,2,256,256]{3,2,1,0:T(8,128)S(1)} %get-tuple-element.8.bypass_ref, bf16[256,512]{1,0:T(8,128)(2,1)S(1)} %copy-done), custom_call_target="tpu_custom_call" | custom-call | flops 100000000 | bytes 1048576 | tf_op jit(solution)/shard_map/to_input_grad/pallas_call | solution.py:332
Async XLA Ops:
  0.6 35.2 %copy-start.2 = (f32[8,8,1,1,32]{4,3,2,1,0:T(1,128)S(1)}, f32[8,8,1,1,32]{4,3,2,1,0:T(1,128)}, u32[]{:S(2)}) copy-start(f32[8,8,1,1,32]{4,3,2,1,0:T(1,128)} %param.10) | copy-start | bytes 24580
  0.6 35.2 %copy-start.3 = (bf16[128,384]{1,0:T(8,128)(2,1)S(1)}, bf16[128,384]{1,0:T(8,128)(2,1)}, u32[]{:S(2)}) copy-start(bf16[128,384]{1,0:T(8,128)(2,1)} %constant.10.clone.back_ref) | copy-start | bytes 294916
  0.7 35.2 %copy-start.4 = (bf16[256,128]{1,0:T(8,128)(2,1)S(1)}, bf16[256,128]{1,0:T(8,128)(2,1)}, u32[]{:S(2)}) copy-start(bf16[256,128]{1,0:T(8,128)(2,1)} %constant.9.clone.depth_ref) | copy-start | bytes 196612
  0.7 49.6 %copy-start.1 = (f32[8,1,1]{0,2,1:T(1,128)S(1)}, f32[8,1,1]{0,2,1:T(1,128)}, u32[]{:S(2)}) copy-start(f32[8,1,1]{0,2,1:T(1,128)} %param.11) | copy-start | bytes 100
  4.1 52.1 %copy-start = (bf16[256,512]{1,0:T(8,128)(2,1)S(1)}, bf16[256,512]{1,0:T(8,128)(2,1)}, u32[]{:S(2)}) copy-start(bf16[256,512]{1,0:T(8,128)(2,1)} %constant.11.clone.table_ref) | copy-start | bytes 786436
  37.1 19.0 %all-to-all-start.1 = ((f32[128,1,128]{2,1,0:T(1,128)}), f32[128,1,128]{2,1,0:T(1,128)S(1)}, u32[]{:S(2)}, u32[]{:S(2)}) async-start(f32[128,1,128]{2,1,0:T(1,128)} %bitcast.6), calls=%async_computation.1 | async-start | bytes 131072 | tf_op jit(solution)/shard_map/all_to_all | solution.py:358
